TPU v7x, 1024 devices: a whole 4x8x16 slice. The times are simulated.
1024 devices in a mesh: ctx: 8 (over y), exp: 16 (over z), etp: 8 (over x, core).
Axes of the slice: x: 4, y: 8, z: 16, core: 2. Of those that a mesh axis runs over, the one named last changes fastest.
Arguments:
- tokens: bfloat16 [4096, 4096], P(('ctx', 'exp'), 'etp'), may hold values from -6 to 6
- grad_out: bfloat16 [4096, 4096], P(('ctx', 'exp'), 'etp'), may hold values from -6 to 6
- route_weight: float32 [4096, 1], P(('ctx', 'exp')), may hold values from 0.1 to 1
- routes: int32 [4096, 1], P(('ctx', 'exp')), may hold values from 0 to 3; in each aligned block of 32 rows (0 to 31, 32 to 63, ...) at most 16 rows name the same one
- w_gate: bfloat16 [21504, 4096], P(('exp', 'etp')), may hold values from -0.09375 to 0.09375
- w_up: bfloat16 [21504, 4096], P(('exp', 'etp')), may hold values from -0.09375 to 0.09375
- w_down: bfloat16 [21504, 4096], P(('exp', 'etp')), may hold values from -0.078125 to 0.078125
Outputs:
- d_tokens: bfloat16 [4096, 4096], P(('ctx', 'exp'), 'etp')
- d_w_gate: bfloat16 [21504, 4096], P(('exp', 'etp'), 'ctx')
- d_w_up: bfloat16 [21504, 4096], P(('exp', 'etp'), 'ctx')
- d_w_down: bfloat16 [21504, 4096], P(('exp', 'etp'), 'ctx')
Inputs may be any that keep to these rules, and one draw needn't show every extreme that they name: `routes`: within each aligned block of 32 tokens (the tokens of one index pair of ctx and exp) at most 16 name the same expert; in every draw some block has exactly 16 naming one expert.
All inputs are finite; a program needn't handle non-finite values.
Results may differ from a plain program's by a relative error of at most 0.02.
Values may be sent and summed in bfloat16 or wider, within the bound.
A program may use at most 64 MiB of HBM per device.

v0:
```python
import jax
import jax.numpy as jnp
from jax import lax
from jax.sharding import PartitionSpec as P

EXPERTS = 4
MOST = 16


def bucket_rows(placement, values, group_split):
    filled = jnp.dot(placement, values, preferred_element_type=jnp.float32).astype(jnp.bfloat16)
    shaped = filled.reshape(EXPERTS, MOST, values.shape[1])
    return jnp.repeat(shaped, group_split, axis=0)


def on_device(tokens, grad_out, route_weight, routes, w_gate, w_up, w_down):
    group_split = lax.axis_size("exp") // EXPERTS
    hid_dev = w_gate.shape[0]
    scaled = (route_weight * grad_out.astype(jnp.float32)).astype(jnp.bfloat16)
    expert_ids = routes[:, 0]
    member = (expert_ids[:, None] == jnp.arange(EXPERTS, dtype=jnp.int32)[None, :]).astype(
        jnp.int32
    )
    ranking = jnp.sum((jnp.cumsum(member, axis=0) - 1) * member, axis=1)
    position = expert_ids * MOST + ranking
    placement = (position[None, :] == jnp.arange(EXPERTS * MOST, dtype=jnp.int32)[:, None]).astype(
        jnp.bfloat16
    )
    full_tokens, full_scaled = (
        lax.all_gather(tokens, "etp", axis=1, tiled=True),
        lax.all_gather(scaled, "etp", axis=1, tiled=True),
    )
    rows_in, grads_in = (
        lax.all_to_all(
            bucket_rows(placement, full_tokens, group_split),
            "exp",
            split_axis=0,
            concat_axis=0,
            tiled=True,
        ),
        lax.all_to_all(
            bucket_rows(placement, full_scaled, group_split),
            "exp",
            split_axis=0,
            concat_axis=0,
            tiled=True,
        ),
    )
    full_width = rows_in.shape[2]
    slot_count = rows_in.shape[0] * rows_in.shape[1]
    rows_in = rows_in.reshape(slot_count, full_width)
    grads_in = grads_in.reshape(slot_count, full_width)
    across = (((1,), (1,)), ((), ()))
    gate_pre = lax.dot_general(rows_in, w_gate, across, preferred_element_type=jnp.float32)
    up_pre = lax.dot_general(rows_in, w_up, across, preferred_element_type=jnp.float32)
    gate_sigmoid = jax.nn.sigmoid(gate_pre)
    activated = gate_pre * gate_sigmoid
    hidden = (activated * up_pre).astype(jnp.bfloat16)
    d_hidden = lax.dot_general(grads_in, w_down, across, preferred_element_type=jnp.float32)
    d_gate_act = (
        d_hidden * up_pre * gate_sigmoid * (1.0 + gate_pre * (1.0 - gate_sigmoid))
    ).astype(jnp.bfloat16)
    d_up_act = (d_hidden * activated).astype(jnp.bfloat16)
    d_slots = jnp.dot(d_gate_act, w_gate, preferred_element_type=jnp.float32) + jnp.dot(
        d_up_act, w_up, preferred_element_type=jnp.float32
    )
    partial_value = d_slots.reshape(-1, MOST, full_width)
    returned = lax.all_to_all(
        partial_value.astype(jnp.bfloat16), "exp", split_axis=0, concat_axis=0, tiled=True
    ).astype(partial_value.dtype)
    merged = (
        returned.reshape(EXPERTS, group_split, MOST, full_width)
        .sum(axis=1)
        .reshape(EXPERTS * MOST, full_width)
    )
    token_rows = jnp.take(merged, position, axis=0)
    d_tokens = lax.psum_scatter(
        token_rows.astype(jnp.bfloat16), "etp", scatter_dimension=1, tiled=True
    )
    leading = (((0,), (0,)), ((), ()))
    weight_sums = lax.psum_scatter(
        jnp.concatenate(
            [
                lax.dot_general(rows_in, d_gate_act, leading, preferred_element_type=jnp.float32),
                lax.dot_general(rows_in, d_up_act, leading, preferred_element_type=jnp.float32),
                lax.dot_general(grads_in, hidden, leading, preferred_element_type=jnp.float32),
            ],
            axis=1,
        ).astype(jnp.bfloat16),
        "ctx",
        scatter_dimension=0,
        tiled=True,
    ).astype(jnp.float32)
    d_w_gate = weight_sums[:, :hid_dev].T.astype(jnp.bfloat16)
    d_w_up = weight_sums[:, hid_dev : 2 * hid_dev].T.astype(jnp.bfloat16)
    d_w_down = weight_sums[:, 2 * hid_dev :].T.astype(jnp.bfloat16)
    return (d_tokens, d_w_gate, d_w_up, d_w_down)


def solution(mesh):
    in_specs = (
        P(("ctx", "exp"), "etp"),
        P(("ctx", "exp"), "etp"),
        P(("ctx", "exp"), None),
        P(("ctx", "exp"), None),
        P(("exp", "etp"), None),
        P(("exp", "etp"), None),
        P(("exp", "etp"), None),
    )
    out_specs = (
        P(("ctx", "exp"), "etp"),
        P(("exp", "etp"), "ctx"),
        P(("exp", "etp"), "ctx"),
        P(("exp", "etp"), "ctx"),
    )
    return jax.shard_map(
        on_device, mesh=mesh, in_specs=in_specs, out_specs=out_specs, check_vma=False
    )
```

profile of v0, /device:TPU:1, one launch (start us, length us, event | category | flops | bytes accessed | tf_op | source)
XLA Modules:
  0.0 407.7 jit_solution(15436457078840963298)
XLA Ops:
  7.2 0.0 copy-start
  7.2 0.8 fusion.5
  8.0 0.1 reduce_window_sum.11
  8.1 0.8 select_reduce_fusion
  8.9 0.7 multiply_add_fusion
  9.6 27.0 %all_gather.7 = bf16[32,4096]{1,0:T(8,128)(2,1)S(1)} all-gather(bf16[32,512]{1,0:T(8,128)(2,1)} %param.7), channel_id=1, replica_groups=mesh['ctx'=8,'exp'=16,'etp'=8] {'etp'}, dimensions={1}, use_global_device_ids=true | all-gather | bytes 294912 | tf_op jit(solution)/shard_map/all_gather | solution.py:30
  36.6 0.3 convolution_convert_fusion.3
  36.9 1.6 broadcast_in_dim.21
  38.4 0.0 copy-start.7
  38.4 0.0 copy-start.9
  38.4 6.4 %all-to-all-start.1 = ((bf16[16,16,4096]{2,1,0:T(8,128)(2,1)}), bf16[16,16,4096]{2,1,0:T(8,128)(2,1)S(1)}, u32[]{:S(2)}, u32[]{:S(2)}) async-start(bf16[16,16,4096]{2,1,0:T(8,128)(2,1)} %bitcast.51), calls=%async_computation.1 | async-start | bytes 4194304 | tf_op jit(solution)/shard_map/all_to_all | solution.py:34
  44.9 0.0 copy-done.7
  44.9 0.0 copy-done.9
  44.9 0.1 multiply_convert_fusion.4
  45.0 13.1 %all_gather.6 = bf16[32,4096]{1,0:T(8,128)(2,1)S(1)} all-gather(bf16[32,512]{1,0:T(8,128)(2,1)S(1)} %multiply_convert_fusion.4), channel_id=1, replica_groups=mesh['ctx'=8,'exp'=16,'etp'=8] {'etp'}, dimensions={1}, use_global_device_ids=true | all-gather | bytes 294912 | tf_op jit(solution)/shard_map/all_gather | solution.py:31
  58.1 1.1 convolution_convert_fusion.4
  59.2 77.7 %all-to-all-done.1 = bf16[16,16,4096]{2,1,0:T(8,128)(2,1)S(1)} async-done(((bf16[16,16,4096]{2,1,0:T(8,128)(2,1)}), bf16[16,16,4096]{2,1,0:T(8,128)(2,1)S(1)}, u32[]{:S(2)}, u32[]{:S(2)}) %all-to-all-start.1) | async-done | bytes 2097184 | tf_op jit(solution)/shard_map/all_to_all | solution.py:34
  136.9 2.6 broadcast_in_dim.20
  139.5 11.1 %all-to-all-start = ((bf16[16,16,4096]{2,1,0:T(8,128)(2,1)}), bf16[16,16,4096]{2,1,0:T(8,128)(2,1)}, u32[]{:S(2)}, u32[]{:S(2)}) async-start(bf16[16,16,4096]{2,1,0:T(8,128)(2,1)} %bitcast.52), calls=%async_computation | async-start | bytes 4194304 | tf_op jit(solution)/shard_map/all_to_all | solution.py:41
  150.6 2.9 fusion.7
  153.4 0.0 copy-done
  153.4 1.5 fusion.8
  155.0 87.6 %all-to-all-done = bf16[16,16,4096]{2,1,0:T(8,128)(2,1)} async-done(((bf16[16,16,4096]{2,1,0:T(8,128)(2,1)}), bf16[16,16,4096]{2,1,0:T(8,128)(2,1)}, u32[]{:S(2)}, u32[]{:S(2)}) %all-to-all-start) | async-done | bytes 2097184 | tf_op jit(solution)/shard_map/all_to_all | solution.py:41
  242.5 0.0 copy-start.4
  242.5 0.0 copy-start.5
  242.5 0.0 copy-start.10
  242.5 3.4 convolution_convert_fusion
  245.9 0.0 copy-done.4
  245.9 0.0 copy-done.5
  245.9 0.0 copy-done.10
  246.0 2.5 multiply_convert_fusion.1
  248.4 0.0 copy-start.6
  248.4 1.6 convolution_convert_fusion.1
  250.0 0.0 copy-done.6
  250.0 0.0 copy-start.3
  250.0 0.7 fusion.9
  250.8 0.6 copy-done.3
  251.4 2.2 fusion
  253.5 11.2 %all-to-all-start.2 = ((bf16[16,16,4096]{2,1,0:T(8,128)(2,1)}), bf16[16,16,4096]{2,1,0:T(8,128)(2,1)}, u32[]{:S(2)}, u32[]{:S(2)}) async-start(bf16[16,16,4096]{2,1,0:T(8,128)(2,1)} %bitcast.50), calls=%async_computation.2 | async-start | bytes 4194304 | tf_op jit(solution)/shard_map/all_to_all | solution.py:68
  264.8 0.0 reduce-scatter.5.cloned.1.call-start
  264.8 0.0 copy-start.1
  264.8 0.0 copy-start.2
  264.8 1.6 convolution_convert_fusion.2
  266.4 0.0 copy-done.1
  266.4 0.2 copy-done.2
  266.6 2.1 pad_maximum_fusion
  268.7 0.0 copy-start.8
  268.7 0.0 reduce-scatter.5.cloned.1.call-update
  268.7 0.0 reduce-scatter.3.cloned.1.call-start
  268.8 0.6 copy-done.8
  269.4 87.3 %all-to-all-done.2 = bf16[16,16,4096]{2,1,0:T(8,128)(2,1)} async-done(((bf16[16,16,4096]{2,1,0:T(8,128)(2,1)}), bf16[16,16,4096]{2,1,0:T(8,128)(2,1)}, u32[]{:S(2)}, u32[]{:S(2)}) %all-to-all-start.2) | async-done | bytes 2097184 | tf_op jit(solution)/shard_map/all_to_all | solution.py:68
  356.7 1.9 convert_reduce_fusion
  358.6 0.7 gather_fusion
  359.3 0.8 select_convert_fusion
  360.1 0.0 reduce-scatter.3.cloned.1.call-update
  360.2 0.0 reduce-scatter.5.cloned.1.call-done
  360.2 1.9 slice_bitcast_fusion
  362.1 38.8 %reduce-scatter.3.cloned.1.call-done = bf16[32,512]{1,0:T(8,128)(2,1)} async-done(((bf16[32,4096]{1,0:T(8,128)(2,1)}), bf16[32,512]{1,0:T(8,128)(2,1)}) %reduce-scatter.3.cloned.1.call-update) | async-done | bytes 32784 | tf_op jit(solution)/shard_map/reduce_scatter | solution.py:77
  (2 shorter events, 0.0 us)
Async XLA Ops:
  7.2 146.3 %copy-start = (bf16[168,4096]{1,0:T(8,128)(2,1)S(1)}, bf16[168,4096]{1,0:T(8,128)(2,1)}, u32[]{:S(2)}) copy-start(bf16[168,4096]{1,0:T(8,128)(2,1)} %param.11) | copy-start | bytes 4128772
  38.4 6.4 %copy-start.7 = (bf16[32,512]{1,0:T(8,128)(2,1)S(1)}, bf16[32,512]{1,0:T(8,128)(2,1)}, u32[]{:S(2)}) copy-start(bf16[32,512]{1,0:T(8,128)(2,1)} %param.8) | copy-start | bytes 98308
  38.4 6.4 %copy-start.9 = (f32[32,1]{0,1:T(1,128)S(1)}, f32[32,1]{0,1:T(1,128)}, u32[]{:S(2)}) copy-start(f32[32,1]{0,1:T(1,128)} %param.9) | copy-start | bytes 388
  38.4 98.5 %all-to-all-start.1 = ((bf16[16,16,4096]{2,1,0:T(8,128)(2,1)}), bf16[16,16,4096]{2,1,0:T(8,128)(2,1)S(1)}, u32[]{:S(2)}, u32[]{:S(2)}) async-start(bf16[16,16,4096]{2,1,0:T(8,128)(2,1)} %bitcast.51), calls=%async_computation.1 | async-start | bytes 4194304 | tf_op jit(solution)/shard_map/all_to_all | solution.py:34
  139.5 103.0 %all-to-all-start = ((bf16[16,16,4096]{2,1,0:T(8,128)(2,1)}), bf16[16,16,4096]{2,1,0:T(8,128)(2,1)}, u32[]{:S(2)}, u32[]{:S(2)}) async-start(bf16[16,16,4096]{2,1,0:T(8,128)(2,1)} %bitcast.52), calls=%async_computation | async-start | bytes 4194304 | tf_op jit(solution)/shard_map/all_to_all | solution.py:41
  242.5 3.4 copy-start.4
  242.5 3.4 copy-start.5
  242.5 3.4 copy-start.10
  248.4 1.6 copy-start.6
  250.0 1.3 copy-start.3
  253.5 103.1 %all-to-all-start.2 = ((bf16[16,16,4096]{2,1,0:T(8,128)(2,1)}), bf16[16,16,4096]{2,1,0:T(8,128)(2,1)}, u32[]{:S(2)}, u32[]{:S(2)}) async-start(bf16[16,16,4096]{2,1,0:T(8,128)(2,1)} %bitcast.50), calls=%async_computation.2 | async-start | bytes 4194304 | tf_op jit(solution)/shard_map/all_to_all | solution.py:68
  264.8 95.4 %reduce-scatter.5.cloned.1.call-start = ((), (), s32[]{:S(2)}) async-start(), calls=%async_computation.6 | async-start | bytes 4644864 | tf_op jit(solution)/shard_map/reduce_scatter | solution.py:81
  264.8 1.6 copy-start.1
  264.8 1.8 copy-start.2
  268.7 0.7 copy-start.8
  268.7 132.2 %reduce-scatter.3.cloned.1.call-start = ((), (), s32[]{:S(2)}) async-start(), calls=%async_computation.5 | async-start | bytes 294912 | tf_op jit(solution)/shard_map/reduce_scatter | solution.py:77
Sparse Core Ops, SparseCore 0:
  269.0 62.5 reduce-scatter.4
  360.3 40.5 reduce-scatter.2
where the time goes:
time: 408 us
  waiting for transfers between devices  291 us (71%)
  blocking collectives  40.1 us (10%)
  starting transfers between devices  28.8 us (7%)
  matrix products  17.7 us (4%)
  between operations  14.2 us (3%)
  local copies, waits for them, and re-layouts  8.18 us (2%)
  other arithmetic  7.31 us (2%)
    all_to_all x1, waiting for transfers between devices, on_device(): lax.all_to_all(bucket_rows(placement, full_scaled, group_split), 'exp', s...  87.6 us
    all_to_all x1, waiting for transfers between devices, on_device(): lax.all_to_all(partial_value.astype(jnp.bfloat16), 'exp', split_axis=0, c...  87.3 us
    all_to_all x1, waiting for transfers between devices, on_device(): lax.all_to_all(bucket_rows(placement, full_tokens, group_split), 'exp', s...  77.7 us
    reduce_scatter x1, waiting for transfers between devices, on_device(): lax.psum_scatter(token_rows.astype(jnp.bfloat16), 'etp', scatter_dimensio...  38.8 us
    all_gather x1, blocking collectives, on_device(): lax.all_gather(tokens, 'etp', axis=1, tiled=True)  27 us
    all_gather x1, blocking collectives, on_device(): lax.all_gather(scaled, 'etp', axis=1, tiled=True)  13.1 us
    all_to_all x1, starting transfers between devices, on_device(): lax.all_to_all(partial_value.astype(jnp.bfloat16), 'exp', split_axis=0, c...  11.2 us
    all_to_all x1, starting transfers between devices, on_device(): lax.all_to_all(bucket_rows(placement, full_scaled, group_split), 'exp', s...  11.1 us
  transfers between devices with their start and end apart: 5, of which 4 were waited for; matrix products, arithmetic and copies ran while one was open for 4% of the time, Pallas kernels for 0%

commit v1 on v0

v1 whole, which is shorter than its diff:
```python
import jax
import jax.numpy as jnp
from jax import lax
from jax.sharding import PartitionSpec as P

EXPERTS = 4
MOST = 16


def on_device(tokens, grad_out, route_weight, routes, w_gate, w_up, w_down):
    n_exp = lax.axis_size("exp")
    group_split = n_exp // EXPERTS
    rows = tokens.shape[0]
    feats = tokens.shape[1]
    hid_dev = w_gate.shape[0]
    my_expert = lax.axis_index("exp") // group_split
    scaled = (route_weight * grad_out.astype(jnp.float32)).astype(jnp.bfloat16)
    tagged = jnp.broadcast_to(routes.astype(jnp.bfloat16), (rows, 128))
    packed = lax.all_gather(
        jnp.concatenate([tokens, scaled, tagged], axis=1), "exp", axis=0, tiled=True
    )
    expert_all = packed[:, 2 * feats].astype(jnp.int32).reshape(n_exp, rows)
    mine = (expert_all == my_expert).astype(jnp.int32)
    rank = jnp.cumsum(mine, axis=1) - 1
    slot = jnp.where(mine == 1, rank, -1)
    pick = (slot[:, None, :] == jnp.arange(MOST, dtype=jnp.int32)[None, :, None]).astype(jnp.bfloat16)
    chosen = lax.dot_general(
        pick,
        packed[:, : 2 * feats].reshape(n_exp, rows, 2 * feats),
        (((2,), (1,)), ((0,), (0,))),
        preferred_element_type=jnp.float32,
    ).astype(jnp.bfloat16)
    slots = n_exp * MOST
    chosen = chosen.reshape(slots, 2, feats)
    full = lax.all_gather(chosen, "etp", axis=0, tiled=False)
    full_t = full.transpose(2, 1, 0, 3).reshape(2, slots, -1)
    rows_in, grads_in = full_t[0], full_t[1]
    full_width = rows_in.shape[1]
    across = (((1,), (1,)), ((), ()))
    gate_pre = lax.dot_general(rows_in, w_gate, across, preferred_element_type=jnp.float32)
    up_pre = lax.dot_general(rows_in, w_up, across, preferred_element_type=jnp.float32)
    gate_sigmoid = jax.nn.sigmoid(gate_pre)
    activated = gate_pre * gate_sigmoid
    hidden = (activated * up_pre).astype(jnp.bfloat16)
    d_hidden = lax.dot_general(grads_in, w_down, across, preferred_element_type=jnp.float32)
    d_gate_act = (
        d_hidden * up_pre * gate_sigmoid * (1.0 + gate_pre * (1.0 - gate_sigmoid))
    ).astype(jnp.bfloat16)
    d_up_act = (d_hidden * activated).astype(jnp.bfloat16)
    d_slots = jnp.dot(d_gate_act, w_gate, preferred_element_type=jnp.float32) + jnp.dot(
        d_up_act, w_up, preferred_element_type=jnp.float32
    )
    part = lax.psum_scatter(d_slots.astype(jnp.bfloat16), "etp", scatter_dimension=1, tiled=True)
    returned = lax.all_to_all(
        part.reshape(n_exp, MOST, feats), "exp", split_axis=0, concat_axis=0, tiled=True
    ).astype(jnp.float32)
    merged = (
        returned.reshape(EXPERTS, group_split, MOST, feats)
        .sum(axis=1)
        .reshape(EXPERTS * MOST, feats)
        .astype(jnp.bfloat16)
    )
    expert_ids = routes[:, 0]
    member = (expert_ids[:, None] == jnp.arange(EXPERTS, dtype=jnp.int32)[None, :]).astype(jnp.int32)
    ranking = jnp.sum((jnp.cumsum(member, axis=0) - 1) * member, axis=1)
    position = expert_ids * MOST + ranking
    place = (position[:, None] == jnp.arange(EXPERTS * MOST, dtype=jnp.int32)[None, :]).astype(jnp.bfloat16)
    d_tokens = jnp.dot(place, merged, preferred_element_type=jnp.float32).astype(jnp.bfloat16)
    leading = (((0,), (0,)), ((), ()))
    weight_sums = lax.psum_scatter(
        jnp.concatenate(
            [
                lax.dot_general(rows_in, d_gate_act, leading, preferred_element_type=jnp.float32),
                lax.dot_general(rows_in, d_up_act, leading, preferred_element_type=jnp.float32),
                lax.dot_general(grads_in, hidden, leading, preferred_element_type=jnp.float32),
            ],
            axis=1,
        ).astype(jnp.bfloat16),
        "ctx",
        scatter_dimension=0,
        tiled=True,
    ).astype(jnp.float32)
    d_w_gate = weight_sums[:, :hid_dev].T.astype(jnp.bfloat16)
    d_w_up = weight_sums[:, hid_dev : 2 * hid_dev].T.astype(jnp.bfloat16)
    d_w_down = weight_sums[:, 2 * hid_dev :].T.astype(jnp.bfloat16)
    return (d_tokens, d_w_gate, d_w_up, d_w_down)


def solution(mesh):
    in_specs = (
        P(("ctx", "exp"), "etp"),
        P(("ctx", "exp"), "etp"),
        P(("ctx", "exp"), None),
        P(("ctx", "exp"), None),
        P(("exp", "etp"), None),
        P(("exp", "etp"), None),
        P(("exp", "etp"), None),
    )
    out_specs = (
        P(("ctx", "exp"), "etp"),
        P(("exp", "etp"), "ctx"),
        P(("exp", "etp"), "ctx"),
        P(("exp", "etp"), "ctx"),
    )
    return jax.shard_map(
        on_device, mesh=mesh, in_specs=in_specs, out_specs=out_specs, check_vma=False
    )
```

time: 408 us -> 267 us (0.65)
  waiting for transfers between devices: 291 us -> 202 us
  starting transfers between devices: 28.8 us -> 0.16 us
  blocking collectives: 40.1 us -> 23.1 us
  matrix products: 17.7 us -> 9.08 us
    all_to_all x3 -> x0, waiting for transfers between devices: 253 us -> none  [the longest x1 87.6 us: on_device(): lax.all_to_all(bucket_rows(placement, full_scaled, group_split), 'exp', s...]
    all_gather x0 -> x2, waiting for transfers between devices: none -> 124 us  [the longest x1 74.4 us: on_device(): lax.all_gather(jnp.concatenate([tokens, scaled, tagged], axis=1), 'exp',...]
    reduce_scatter x1, waiting for transfers between devices: 0.02 us -> 41.2 us  [on_device(): lax.psum_scatter(jnp.concatenate([lax.dot_general(rows_in, d_gate_act, le...]
    all_gather x2 -> x0, blocking collectives: 40.1 us -> none  [the longest x1 27 us: on_device(): lax.all_gather(tokens, 'etp', axis=1, tiled=True)]
    all_to_all x3 -> x0, starting transfers between devices: 28.7 us -> none  [the longest x1 11.2 us: on_device(): lax.all_to_all(partial_value.astype(jnp.bfloat16), 'exp', split_axis=0, c...]
    all_to_all x0 -> x1, blocking collectives: none -> 23.1 us  [on_device(): lax.all_to_all(part.reshape(n_exp, MOST, feats), 'exp', split_axis=0, con...]
    broadcast_in_dim x2 -> x1, local copies, waits for them, and re-layouts: 4.18 us -> 0.07 us  [on_device(): tagged = jnp.broadcast_to(routes.astype(jnp.bfloat16), (rows, 128))]
  transfers between devices with their start and end apart: 5 -> 4, of which waited for: 4 -> 4; matrix products, arithmetic and copies ran while one was open for 4% -> 2% of each run, Pallas kernels for 0% -> 0%
where the time goes in v1:
time: 267 us; the launch traced here: 266 us
  waiting for transfers between devices  202 us (76%)
  blocking collectives  23.1 us (9%)
  between operations  14 us (5%)
  local copies, waits for them, and re-layouts  9.31 us (3%)
  matrix products  9.08 us (3%)
  other arithmetic  8.22 us (3%)
    all_gather x1, waiting for transfers between devices, on_device(): lax.all_gather(jnp.concatenate([tokens, scaled, tagged], axis=1), 'exp',...  74.4 us
    all_gather x1, waiting for transfers between devices, on_device(): full = lax.all_gather(chosen, 'etp', axis=0, tiled=False)  49.1 us
    reduce_scatter x1, waiting for transfers between devices, on_device(): lax.psum_scatter(jnp.concatenate([lax.dot_general(rows_in, d_gate_act, le...  41.2 us
    reduce_scatter x1, waiting for transfers between devices, on_device(): lax.psum_scatter(d_slots.astype(jnp.bfloat16), 'etp', scatter_dimension=1...  37.3 us
    all_to_all x1, blocking collectives, on_device(): lax.all_to_all(part.reshape(n_exp, MOST, feats), 'exp', split_axis=0, con...  23.1 us
  transfers between devices with their start and end apart: 4, of which 4 were waited for; matrix products, arithmetic and copies ran while one was open for 2% of the time, Pallas kernels for 0%

profile of v1, /device:TPU:1, one launch (start us, length us, event | category | flops | bytes accessed | tf_op | source)
XLA Modules:
  0.0 265.9 jit_solution(6282913906776489361)
XLA Ops:
  7.2 0.0 copy-start
  7.2 0.0 all-gather.3.cloned.1.call-start
  7.2 0.8 fusion.4
  8.1 0.1 reduce_window_sum.22
  8.1 0.8 select_reduce_fusion
  8.9 0.7 fusion.6
  9.7 0.8 multiply_convert_fusion.4
  10.5 0.1 broadcast_in_dim.7
  10.6 1.4 pad_maximum_fusion.1
  12.0 0.0 all-gather.3.cloned.1.call-update
  12.0 0.0 all-gather.5.cloned.1.call-start
  12.1 74.4 %all-gather.3.cloned.1.call-done = bf16[512,1152]{1,0:T(8,128)(2,1)} async-done(((bf16[32,1152]{1,0:T(8,128)(2,1)}), bf16[512,1152]{1,0:T(8,128)(2,1)}) %all-gather.3.cloned.1.call-update) | async-done | bytes 1179664 | tf_op jit(solution)/shard_map/all_gather | solution.py:19
  86.5 0.0 slice-start
  86.5 1.1 convert_reduce_fusion
  87.6 0.1 reshape.61
  87.7 0.2 reduce_window_sum.23
  87.9 0.0 slice-done
  87.9 0.3 convolution_convert_fusion.3
  88.2 0.4 all_gather_reshape.3
  88.6 1.2 copy.11
  89.8 0.0 all-gather.5.cloned.1.call-update
  89.8 0.0 reduce-scatter.3.cloned.1.call-start
  89.9 49.1 %all-gather.5.cloned.1.call-done = bf16[8,256,2,512]{1,3,0,2:T(8,128)(2,1)} async-done(((bf16[1,256,2,512]{1,3,0,2:T(8,128)(2,1)}), bf16[8,256,2,512]{1,3,0,2:T(8,128)(2,1)}) %all-gather.5.cloned.1.call-update) | async-done | bytes 4194320 | tf_op jit(solution)/shard_map/all_gather | solution.py:35
  139.0 2.6 fusion.8
  141.6 0.0 copy-start.1
  141.6 0.0 copy-start.3
  141.6 0.0 copy-done
  141.6 0.5 fusion.10
  142.1 1.5 copy-done.3
  143.7 0.0 copy-start.4
  143.7 0.0 copy-start.11
  143.7 0.6 fusion.9
  144.2 0.0 copy-start.6
  144.3 0.0 copy-done.1
  144.3 0.8 copy-done.11
  145.1 0.5 multiply_convert_fusion.1
  145.6 0.0 copy-done.4
  145.6 0.0 copy-done.6
  145.6 0.0 copy-start.8
  145.6 0.0 copy-start.10
  145.7 0.7 fusion.11
  146.4 0.0 copy-done.8
  146.4 0.0 copy-done.10
  146.4 2.1 fusion
  148.6 0.0 reduce-scatter.3.cloned.1.call-update
  148.6 0.0 reduce-scatter.5.cloned.1.call-start
  148.6 0.0 copy-start.9
  148.6 1.8 convolution_convert_fusion.1
  150.4 0.0 copy-done.9
  150.4 0.0 copy-start.2
  150.4 0.0 copy-start.5
  150.4 0.0 copy-start.7
  150.5 0.8 convolution_convert_fusion.2
  151.3 0.7 copy-done.2
  152.0 0.0 copy-done.5
  152.0 0.0 copy-done.7
  152.0 0.9 convolution_convert_fusion
  152.9 2.2 pad_maximum_fusion
  155.0 0.0 reduce-scatter.5.cloned.1.call-update
  155.1 37.3 %reduce-scatter.3.cloned.1.call-done = bf16[256,512]{1,0:T(8,128)(2,1)} async-done(((bf16[256,4096]{1,0:T(8,128)(2,1)}), bf16[256,512]{1,0:T(8,128)(2,1)}) %reduce-scatter.3.cloned.1.call-update) | async-done | bytes 262160 | tf_op jit(solution)/shard_map/reduce_scatter | solution.py:53
  192.4 23.1 %all_to_all.5 = bf16[16,16,512]{2,1,0:T(8,128)(2,1)S(1)} all-to-all(bf16[16,16,512]{2,1,0:T(8,128)(2,1)} %bitcast.50), channel_id=1, replica_groups=mesh['ctx'=8,'exp'=16,'etp'=8] {'exp'}, dimensions={0} | all-to-all | bytes 524288 | tf_op jit(solution)/shard_map/all_to_all | solution.py:54
  215.5 0.8 convolution_convert_fusion.4
  216.3 41.2 %reduce-scatter.5.cloned.1.call-done = bf16[512,504]{0,1:T(8,128)(2,1)} async-done(((bf16[4096,504]{0,1:T(8,128)(2,1)}), bf16[512,504]{0,1:T(8,128)(2,1)}) %reduce-scatter.5.cloned.1.call-update) | async-done | bytes 516112 | tf_op jit(solution)/shard_map/reduce_scatter | solution.py:70
  257.5 1.9 slice_bitcast_fusion
  (2 shorter events, 0.0 us)
Async XLA Ops:
  7.2 134.4 %copy-start = (bf16[168,4096]{1,0:T(8,128)(2,1)S(1)}, bf16[168,4096]{1,0:T(8,128)(2,1)}, u32[]{:S(2)}) copy-start(bf16[168,4096]{1,0:T(8,128)(2,1)} %param.11) | copy-start | bytes 4128772
  7.2 79.3 %all-gather.3.cloned.1.call-start = ((), (), s32[]{:S(2)}) async-start(), calls=%async_computation.3 | async-start | bytes 1253376 | tf_op jit(solution)/shard_map/all_gather | solution.py:19
  12.0 127.0 %all-gather.5.cloned.1.call-start = ((), (), s32[]{:S(2)}) async-start(), calls=%async_computation.4 | async-start | bytes 4718592 | tf_op jit(solution)/shard_map/all_gather | solution.py:35
  86.5 1.4 slice-start
  89.8 102.6 %reduce-scatter.3.cloned.1.call-start = ((), (), s32[]{:S(2)}) async-start(), calls=%async_computation.5 | async-start | bytes 2359296 | tf_op jit(solution)/shard_map/reduce_scatter | solution.py:53
  141.6 2.7 %copy-start.1 = (bf16[1,256,8,512]{1,3,2,0:T(8,128)(2,1)}, bf16[1,256,8,512]{1,3,2,0:T(8,128)(2,1)S(1)}, u32[]{:S(2)}) copy-start(bf16[1,256,8,512]{1,3,2,0:T(8,128)(2,1)S(1)} %get-tuple-element.4) | copy-start | bytes 6291460
  141.6 2.1 copy-start.3
  143.7 2.0 copy-start.4
  143.7 1.4 copy-start.11
  144.2 1.4 copy-start.6
  145.6 0.8 copy-start.8
  145.6 0.8 copy-start.10
  148.6 109.0 %reduce-scatter.5.cloned.1.call-start = ((), (), s32[]{:S(2)}) async-start(), calls=%async_computation.6 | async-start | bytes 4644864 | tf_op jit(solution)/shard_map/reduce_scatter | solution.py:70
  148.6 1.8 copy-start.9
  150.4 1.6 copy-start.2
  150.4 1.6 copy-start.5
  150.4 1.6 copy-start.7
Sparse Core Ops, SparseCore 0:
  12.1 74.2 all-gather.2
  89.9 48.9 all-gather.4
  148.7 43.6 reduce-scatter.2
  195.7 61.7 reduce-scatter.4

commit v2 on v1

v2 whole, which is shorter than its diff:
```python
import functools

import jax
import jax.numpy as jnp
from jax import lax
from jax.experimental import pallas as pl
from jax.experimental.pallas import tpu as pltpu
from jax.sharding import PartitionSpec as P

EXPERTS = 4
MOST = 16
TAG = 128
LANES = 4
LAG_NEAR = 2
LAG_FAR = 4
MESH = pl.DeviceIdType.MESH
F32 = jnp.float32
BF16 = jnp.bfloat16
ACROSS = (((1,), (1,)), ((), ()))
LEADING = (((0,), (0,)), ((), ()))


def aligned(index, size):
    return pl.ds(pl.multiple_of(index * size, size), size)


def kernel(
    n_ctx,
    n_exp,
    n_etp,
    tok_ref,
    grad_ref,
    weight_ref,
    routes_ref,
    gate_hbm,
    up_hbm,
    down_hbm,
    d_tok_ref,
    d_gate_ref,
    d_up_ref,
    d_down_ref,
    raw,
    x,
    w_gate,
    w_up,
    w_down,
    acts,
    total,
    y_out,
    y_in,
    pair_out,
    pair_in,
    far_out,
    far_in,
    near_sum,
    near_out,
    near_in,
    home_out,
    home_in,
    w_sem,
    z_send,
    z_recv,
    x_send,
    x_recv,
    y_send,
    y_recv,
    pair_send,
    pair_recv,
    far_send,
    far_recv,
    near_send,
    near_recv,
    home_send,
    home_recv,
):
    rows, feats = tok_ref.shape
    hid = w_gate.shape[0]
    half = rows // 2
    n_x = n_etp // 2
    group_split = n_exp // EXPERTS
    chunks = n_exp // 2
    slots = n_exp * MOST
    c = lax.axis_index("ctx")
    z = lax.axis_index("exp")
    t = lax.axis_index("etp")
    xx = t // 2
    core = t % 2
    sib = t + 1 - 2 * core
    expert = z // group_split

    def along_x(step):
        return ((xx + step) % n_x) * 2 + core

    right, left, far = along_x(1), along_x(n_x - 1), along_x(2)
    z_next, z_prev = (z + 1) % n_exp, (z + n_exp - 1) % n_exp
    y_next, y_prev = (c + 1) % n_ctx, (c + n_ctx - 1) % n_ctx

    loads = [
        pltpu.make_async_copy(src, dst, w_sem.at[i])
        for i, (src, dst) in enumerate(((gate_hbm, w_gate), (up_hbm, w_up), (down_hbm, w_down)))
    ]
    for load in loads:
        load.start()

    barrier = pltpu.get_barrier_semaphore()
    partners = [{"etp": right}, {"etp": left}, {"etp": sib}, {"ctx": y_next}, {"ctx": y_prev}]
    partners += [{"exp": (z + k) % n_exp} for k in range(1, n_exp)]
    for partner in partners:
        pl.semaphore_signal(barrier, inc=1, device_id=partner, device_id_type=MESH)

    expert_col = routes_ref[...]
    lane = lax.broadcasted_iota(jnp.int32, (rows, TAG), 1)
    one_hot = (lane == expert_col).astype(BF16)
    earlier = (
        lax.broadcasted_iota(jnp.int32, (rows, rows), 0)
        > lax.broadcasted_iota(jnp.int32, (rows, rows), 1)
    ).astype(BF16)
    before = jnp.dot(earlier, one_hot, preferred_element_type=F32)
    rank = jnp.sum(before * one_hot.astype(F32), axis=1, keepdims=True)
    position = expert_col.astype(F32) * MOST + rank
    raw[:rows, :feats] = tok_ref[...]
    raw[:rows, feats : 2 * feats] = (weight_ref[...] * grad_ref[...].astype(F32)).astype(BF16)
    raw[:rows, 2 * feats :] = jnp.broadcast_to(position, (rows, TAG)).astype(BF16)

    pl.semaphore_wait(barrier, len(partners))

    def send(src, dst, send_sem, recv_sem, target):
        return pltpu.make_async_remote_copy(
            src_ref=src,
            dst_ref=dst,
            send_sem=send_sem,
            recv_sem=recv_sem,
            device_id=target,
            device_id_type=MESH,
        )

    def raw_half(block, part):
        return raw.at[aligned(2 * block + part, half)]

    def z_copy(src, dst, part, target):
        return send(
            raw_half(src, part),
            raw_half(dst, part),
            z_send.at[dst, part],
            z_recv.at[dst, part],
            {"exp": target},
        )

    for part in range(2):
        z_copy(0, 1, part, z_next).start()
        z_copy(0, 2, part, z_prev).start()

    def piece(k, owner):
        return x.at[:, aligned(k, 2 * MOST), aligned(owner, feats)]

    def piece_of(kind, k, owner):
        return x.at[kind, aligned(k, 2 * MOST), aligned(owner, feats)]

    def x_copy(which, k):
        if which == 0:
            ref, target = piece(k, t), right
        elif which == 1:
            ref, target = piece(k, t), left
        elif which == 2:
            ref, target = piece(k, t), sib
        elif which == 3:
            ref, target = piece_of(0, k, left), right
        elif which == 4:
            ref, target = piece_of(1, k, right), left
        elif which == 5:
            ref, target = piece(k, left), sib
        elif which == 6:
            ref, target = piece(k, right), sib
        elif which == 7:
            ref, target = piece_of(0, k, far), sib
        else:
            ref, target = piece_of(1, k, far), sib
        return send(ref, ref, x_send.at[which, k], x_recv.at[which, k], {"etp": target})

    def x_arrive(which, k):
        turn = 1 - 2 * core
        if which == 0:
            ref = piece(k, left)
        elif which == 1:
            ref = piece(k, right)
        elif which == 2:
            ref = piece(k, sib)
        elif which == 3:
            ref = piece_of(0, k, far)
        elif which == 4:
            ref = piece_of(1, k, far)
        elif which == 5:
            ref = piece(k, left + turn)
        elif which == 6:
            ref = piece(k, right + turn)
        elif which == 7:
            ref = piece_of(0, k, far + turn)
        else:
            ref = piece_of(1, k, far + turn)
        send(ref, ref, x_send.at[which, k], x_recv.at[which, k], {"etp": sib}).wait_recv()

    pick_row = lax.broadcasted_iota(jnp.int32, (2 * rows, 2 * MOST), 0)
    pick_lane = lax.broadcasted_iota(jnp.int32, (2 * rows, 2 * MOST), 1)

    def dispatch(i, carry):
        @pl.when(i < chunks)
        def _():
            forth, back = 2 * i + 1, 2 * i + 2
            for part in range(2):
                z_copy(forth, forth, part, z_next).wait_recv()

                @pl.when(i < chunks - 1)
                def _():
                    z_copy(forth, forth + 2, part, z_next).start()
                    z_copy(back, back, part, z_prev).wait_recv()

                @pl.when(i < chunks - 2)
                def _():
                    z_copy(back, back + 2, part, z_prev).start()

            block = raw[aligned(i, 2 * rows), :]
            tag = block[:, 2 * feats : 2 * feats + 2 * MOST].astype(jnp.int32) - expert * MOST
            spot = jnp.where(pick_row >= rows, tag + MOST, tag)
            pick = jnp.where((tag >= 0) & (tag < MOST) & (spot == pick_lane), 1.0, 0.0).astype(BF16)
            chosen = lax.dot_general(
                pick, block[:, : 2 * feats], LEADING, preferred_element_type=F32
            ).astype(BF16)
            x[0, aligned(i, 2 * MOST), aligned(t, feats)] = chosen[:, :feats]
            x[1, aligned(i, 2 * MOST), aligned(t, feats)] = chosen[:, feats:]
            for which in range(3):
                x_copy(which, i).start()

        @pl.when((i >= LAG_NEAR) & (i < chunks + LAG_NEAR))
        def _():
            k = i - LAG_NEAR
            x_arrive(0, k)
            x_copy(3, k).start()
            x_copy(5, k).start()
            x_arrive(1, k)
            x_copy(4, k).start()
            x_copy(6, k).start()

        @pl.when(i >= LAG_FAR)
        def _():
            k = i - LAG_FAR
            x_arrive(3, k)
            x_copy(7, k).start()
            x_arrive(4, k)
            x_copy(8, k).start()

        return carry

    lax.fori_loop(0, chunks + LAG_FAR, dispatch, 0)

    def gathered(k, carry):
        for which in (2, 5, 6, 7, 8):
            x_arrive(which, k)
        for which in range(9):
            x_copy(which, k).wait_send()
        return carry

    lax.fori_loop(0, chunks, gathered, 0)
    for load in loads:
        load.wait()

    tok_all, grad_all = x[0], x[1]
    gate = lax.dot_general(w_gate[...], tok_all, ACROSS, preferred_element_type=F32)
    up = lax.dot_general(w_up[...], tok_all, ACROSS, preferred_element_type=F32)
    d_hidden = lax.dot_general(w_down[...], grad_all, ACROSS, preferred_element_type=F32)
    sig = jax.nn.sigmoid(gate)
    activated = gate * sig
    hidden = activated * up
    d_gate = d_hidden * up * sig * (1.0 + gate * (1.0 - sig))
    d_up = d_hidden * activated
    acts_rows = acts.shape[0]
    acts[...] = jnp.concatenate(
        [d_gate, d_up, hidden, jnp.zeros((acts_rows - 3 * hid, slots), F32)], axis=0
    ).astype(BF16)
    wide = -(-hid // 128) * 128
    fill = jnp.zeros((wide - hid, slots), F32)
    gate_act = jnp.concatenate([d_gate, fill], axis=0).T.astype(BF16)[:, :hid]
    up_act = jnp.concatenate([d_up, fill], axis=0).T.astype(BF16)[:, :hid]

    lane_rows = acts_rows // LANES

    def weight_part(number, owner):
        low, high = number * lane_rows, (number + 1) * lane_rows
        cols = aligned(owner, feats)
        parts = []
        if low < 2 * hid:
            parts.append(
                jnp.dot(acts[low : min(high, 2 * hid), :], x[0, :, cols], preferred_element_type=F32)
            )
        if high > 2 * hid:
            parts.append(
                jnp.dot(acts[max(low, 2 * hid) : high, :], x[1, :, cols], preferred_element_type=F32)
            )
        return parts[0] if len(parts) == 1 else jnp.concatenate(parts, axis=0)

    def y_copy(number, step):
        target = y_next if number < LANES // 2 else y_prev
        return send(
            y_out.at[number, step],
            y_in.at[number, step],
            y_send.at[number, step],
            y_recv.at[number, step],
            {"ctx": target},
        )

    def y_step(step):
        for number in (0, 2, 1, 3):
            if number < LANES // 2:
                owner = (c + 2 * n_ctx - 1 - step) % n_ctx
            else:
                owner = (c + 1 + step) % n_ctx
            value = weight_part(number, owner)
            if step > 0:
                y_copy(number, step - 1).wait_recv()
                value = value + y_in[number, step - 1].astype(F32)
            y_out[number, step] = value.astype(BF16)
            y_copy(number, step).start()

    def y_last():
        for number in (0, 2, 1, 3):
            value = weight_part(number, c)
            y_copy(number, n_ctx - 2).wait_recv()
            total[number * lane_rows : (number + 1) * lane_rows, :] = value + y_in[
                number, n_ctx - 2
            ].astype(F32)
        d_gate_ref[...] = total[:hid, :].astype(BF16)
        d_up_ref[...] = total[hid : 2 * hid, :].astype(BF16)
        d_down_ref[...] = total[2 * hid : 3 * hid, :].astype(BF16)

    def slot_part(owner):
        cols = aligned(owner, feats)
        return jnp.dot(gate_act, w_gate[:, cols], preferred_element_type=F32) + jnp.dot(
            up_act, w_up[:, cols], preferred_element_type=F32
        )

    def pair_copy(i):
        return send(
            pair_out.at[i], pair_in.at[i], pair_send.at[i], pair_recv.at[i], {"etp": sib}
        )

    middle = slots // 2

    def far_copy(side):
        return send(
            far_out.at[pl.ds(side * middle, middle)],
            far_in.at[side],
            far_send.at[side],
            far_recv.at[side],
            {"etp": left if side else right},
        )

    def near_copy(side):
        return send(
            near_out.at[side],
            near_in.at[side],
            near_send.at[side],
            near_recv.at[side],
            {"etp": left if side else right},
        )

    def to_pair():
        for i in (2, 1, 3, 0):
            pair_out[i] = slot_part(((xx + i) % n_x) * 2 + 1 - core).astype(BF16)
            pair_copy(i).start()

    def pair_sum(i):
        value = slot_part(along_x(i))
        pair_copy(i).wait_recv()
        return value + pair_in[i].astype(F32)

    def to_far():
        far_out[...] = pair_sum(2).astype(BF16)
        far_copy(0).start()
        far_copy(1).start()
        near_sum[0] = pair_sum(1)
        near_sum[1] = pair_sum(n_x - 1)

    def to_near():
        far_copy(0).wait_recv()
        near_out[0, :middle, :] = (near_sum[0, :middle, :] + far_in[0].astype(F32)).astype(BF16)
        near_out[0, middle:, :] = near_sum[0, middle:, :].astype(BF16)
        near_copy(0).start()
        far_copy(1).wait_recv()
        near_out[1, :middle, :] = near_sum[1, :middle, :].astype(BF16)
        near_out[1, middle:, :] = (near_sum[1, middle:, :] + far_in[1].astype(F32)).astype(BF16)
        near_copy(1).start()
        near_sum[2] = pair_sum(0)

    def shift(block):
        k = (block + 1) // 2
        return -k if block % 2 else k

    def home_copy(block):
        return send(
            home_out.at[pl.ds(block * MOST, MOST)],
            home_in.at[z],
            home_send.at[block],
            home_recv.at[block],
            {"exp": (z + shift(block) + n_exp) % n_exp},
        )

    def to_home():
        near_copy(0).wait_recv()
        near_copy(1).wait_recv()
        home_out[...] = (
            near_sum[2] + near_in[0].astype(F32) + near_in[1].astype(F32)
        ).astype(BF16)
        for block in range(1, n_exp):
            home_copy(block).start()
        home_in[z] = home_out[:MOST, :]

    def at_home():
        for block in range(1, n_exp):
            source = (z - shift(block) + n_exp) % n_exp
            ref = home_in.at[source]
            send(ref, ref, home_send.at[block], home_recv.at[block], {"exp": source}).wait_recv()
        merged = []
        for e in range(EXPERTS):
            value = home_in[e * group_split].astype(F32)
            for j in range(1, group_split):
                value = value + home_in[e * group_split + j].astype(F32)
            merged.append(value)
        merged = jnp.concatenate(merged, axis=0).astype(BF16)
        spots = EXPERTS * MOST
        place = jnp.where(
            lax.broadcasted_iota(jnp.int32, (rows, spots), 1) == position.astype(jnp.int32), 1.0, 0.0
        ).astype(BF16)
        d_tok_ref[...] = jnp.dot(place, merged, preferred_element_type=F32).astype(BF16)

    between = {0: to_pair, 1: to_far, 2: to_near, 3: to_home, 5: at_home}
    for step in range(n_ctx - 1):
        y_step(step)
        if step in between:
            between[step]()
    for step in sorted(between):
        if step >= n_ctx - 1:
            between[step]()
    y_last()

    for block in range(1, n_exp):
        for part in range(2):
            z_copy(block, block, part, z_next).wait_send()
        home_copy(block).wait_send()
    for number in range(LANES):
        for step in range(n_ctx - 1):
            y_copy(number, step).wait_send()
    for i in range(n_x):
        pair_copy(i).wait_send()
    for side in range(2):
        far_copy(side).wait_send()
        near_copy(side).wait_send()


def on_device(tokens, grad_out, route_weight, routes, w_gate, w_up, w_down):
    n_ctx, n_exp, n_etp = (lax.axis_size(name) for name in ("ctx", "exp", "etp"))
    rows, feats = tokens.shape
    hid, full = w_gate.shape
    slots = n_exp * MOST
    n_x = n_etp // 2
    chunks = n_exp // 2
    acts_rows = -(-3 * hid // (16 * LANES)) * 16 * LANES
    lane_rows = acts_rows // LANES
    vmem = pl.BlockSpec(memory_space=pltpu.VMEM)
    hbm = pl.BlockSpec(memory_space=pl.ANY)
    dma = pltpu.SemaphoreType.DMA
    steps = n_ctx - 1
    grad_shape = jax.ShapeDtypeStruct((hid, feats), BF16)
    return pl.pallas_call(
        functools.partial(kernel, n_ctx, n_exp, n_etp),
        out_shape=(jax.ShapeDtypeStruct((rows, feats), BF16), grad_shape, grad_shape, grad_shape),
        in_specs=[vmem] * 4 + [hbm] * 3,
        out_specs=(vmem,) * 4,
        scratch_shapes=[
            pltpu.VMEM((n_exp * rows, 2 * feats + TAG), BF16),
            pltpu.VMEM((2, slots, full), BF16),
            pltpu.VMEM((hid, full), BF16),
            pltpu.VMEM((hid, full), BF16),
            pltpu.VMEM((hid, full), BF16),
            pltpu.VMEM((acts_rows, slots), BF16),
            pltpu.VMEM((acts_rows, feats), F32),
            pltpu.VMEM((LANES, steps, lane_rows, feats), BF16),
            pltpu.VMEM((LANES, steps, lane_rows, feats), BF16),
            pltpu.VMEM((n_x, slots, feats), BF16),
            pltpu.VMEM((n_x, slots, feats), BF16),
            pltpu.VMEM((slots, feats), BF16),
            pltpu.VMEM((2, slots // 2, feats), BF16),
            pltpu.VMEM((3, slots, feats), F32),
            pltpu.VMEM((2, slots, feats), BF16),
            pltpu.VMEM((2, slots, feats), BF16),
            pltpu.VMEM((slots, feats), BF16),
            pltpu.VMEM((n_exp, MOST, feats), BF16),
            dma((3,)),
            dma((n_exp, 2)),
            dma((n_exp, 2)),
            dma((9, chunks)),
            dma((9, chunks)),
            dma((LANES, steps)),
            dma((LANES, steps)),
            dma((n_x,)),
            dma((n_x,)),
            dma((2,)),
            dma((2,)),
            dma((2,)),
            dma((2,)),
            dma((n_exp,)),
            dma((n_exp,)),
        ],
        compiler_params=pltpu.CompilerParams(
            collective_id=0, has_side_effects=True, vmem_limit_bytes=48 * 1024 * 1024
        ),
        name="expert_backward",
    )(tokens, grad_out, route_weight, routes, w_gate, w_up, w_down)


def solution(mesh):
    in_specs = (
        P(("ctx", "exp"), "etp"),
        P(("ctx", "exp"), "etp"),
        P(("ctx", "exp"), None),
        P(("ctx", "exp"), None),
        P(("exp", "etp"), None),
        P(("exp", "etp"), None),
        P(("exp", "etp"), None),
    )
    out_specs = (
        P(("ctx", "exp"), "etp"),
        P(("exp", "etp"), "ctx"),
        P(("exp", "etp"), "ctx"),
        P(("exp", "etp"), "ctx"),
    )
    return jax.shard_map(
        on_device, mesh=mesh, in_specs=in_specs, out_specs=out_specs, check_vma=False
    )
```

time: 267 us -> 120 us (0.45)
  waiting for transfers between devices: 202 us -> 0 us
  Pallas kernels: 0 us -> 108 us
  blocking collectives: 23.1 us -> 0 us
  between operations: 14 us -> 0.65 us
  matrix products: 9.08 us -> 0 us
  other arithmetic: 8.22 us -> 0 us
    all_gather x2 -> x0, waiting for transfers between devices: 124 us -> none  [the longest x1 74.4 us: on_device(): lax.all_gather(jnp.concatenate([tokens, scaled, tagged], axis=1), 'exp',...]
    pallas_call x0 -> x1, Pallas kernels: none -> 108 us  [on_device(): pl.pallas_call(functools.partial(kernel, n_ctx, n_exp, n_etp), out_shape=...]
    reduce_scatter x2 -> x0, waiting for transfers between devices: 78.5 us -> none  [the longest x1 41.2 us: on_device(): lax.psum_scatter(jnp.concatenate([lax.dot_general(rows_in, d_gate_act, le...]
    all_to_all x1 -> x0, blocking collectives: 23.1 us -> none  [on_device(): lax.all_to_all(part.reshape(n_exp, MOST, feats), 'exp', split_axis=0, con...]
    dot_general x10 -> x0, matrix products: 9.08 us -> none  [the longest x1 2.14 us: on_device(): jnp.dot(d_up_act, w_up, preferred_element_type=jnp.float32)]
    unnamed x24 -> x16, local copies, waits for them, and re-layouts: 3.12 us -> 9.62 us
    concatenate x2 -> x0, other arithmetic: 3.56 us -> none  [the longest x1 2.16 us: on_device(): jnp.concatenate([lax.dot_general(rows_in, d_gate_act, leading, preferred_...]
    convert_element_type x3 -> x0, other arithmetic: 2.8 us -> none  [the longest x1 1.14 us: on_device(): mine = (expert_all == my_expert).astype(jnp.int32)]
  transfers between devices with their start and end apart: 4 -> 0, of which waited for: 4 -> 0; matrix products, arithmetic and copies ran while one was open for 2% -> 0% of each run, Pallas kernels for 0% -> 0%
where the time goes in v2:
time: 120 us; the launch traced here: 119 us
  Pallas kernels  108 us (90%)
  local copies, waits for them, and re-layouts  9.62 us (8%)
    pallas_call x1, Pallas kernels, on_device(): pl.pallas_call(functools.partial(kernel, n_ctx, n_exp, n_etp), out_shape=...  108 us
    unnamed x16, local copies, waits for them, and re-layouts  9.62 us

profile of v2, /device:TPU:1, one launch (start us, length us, event | category | flops | bytes accessed | tf_op | source)
XLA Modules:
  0.0 118.8 jit_solution(1283033980959437800)
XLA Ops:
  0.6 0.7 copy.11.weight_ref
  1.4 0.7 copy.12.routes_ref
  2.1 0.0 copy-start
  2.1 1.3 %copy-done = bf16[168,4096]{1,0:T(8,128)(2,1)S(1)} copy-done((bf16[168,4096]{1,0:T(8,128)(2,1)S(1)}, bf16[168,4096]{1,0:T(8,128)(2,1)}, u32[]{:S(2)}) %copy-start) | copy-done | bytes 1376280
  3.4 0.0 copy-start.1
  3.4 1.3 %copy-done.1 = bf16[168,4096]{1,0:T(8,128)(2,1)S(1)} copy-done((bf16[168,4096]{1,0:T(8,128)(2,1)S(1)}, bf16[168,4096]{1,0:T(8,128)(2,1)}, u32[]{:S(2)}) %copy-start.1) | copy-done | bytes 1376280
  4.8 0.0 copy-start.2
  4.8 1.3 %copy-done.2 = bf16[168,4096]{1,0:T(8,128)(2,1)S(1)} copy-done((bf16[168,4096]{1,0:T(8,128)(2,1)S(1)}, bf16[168,4096]{1,0:T(8,128)(2,1)}, u32[]{:S(2)}) %copy-start.2) | copy-done | bytes 1376280
  6.1 0.0 copy-start.3
  6.1 0.8 copy-done.3
  6.9 0.0 copy-start.4
  6.9 0.8 copy-done.4
  7.6 108.5 %expert_backward.1 = (bf16[32,512]{1,0:T(8,128)(2,1)S(1)}, bf16[168,512]{1,0:T(8,128)(2,1)S(1)}, bf16[168,512]{1,0:T(8,128)(2,1)S(1)}, bf16[168,512]{1,0:T(8,128)(2,1)S(1)}) custom-call(bf16[32,512]{1,0:T(8,128)(2,1)S(1)} %copy-done.3, bf16[32,512]{1,0:T(8,128)(2,1)S(1)} %copy-done.4, f32[32,1]{1,0:T(8,128)S(1)} %copy.11.weight_ref, ...), custom_call_target="tpu_custom_call" | custom-call | tf_op jit(solution)/shard_map/expert_backward/pallas_call | solution.py:472
  116.1 0.6 copy.17
  116.8 0.7 copy.18
  117.4 0.7 copy.19
  118.1 0.7 copy.20
Async XLA Ops:
  2.1 1.3 %copy-start = (bf16[168,4096]{1,0:T(8,128)(2,1)S(1)}, bf16[168,4096]{1,0:T(8,128)(2,1)}, u32[]{:S(2)}) copy-start(bf16[168,4096]{1,0:T(8,128)(2,1)} %gate_hbm.1) | copy-start | bytes 4128772
  3.4 1.3 %copy-start.1 = (bf16[168,4096]{1,0:T(8,128)(2,1)S(1)}, bf16[168,4096]{1,0:T(8,128)(2,1)}, u32[]{:S(2)}) copy-start(bf16[168,4096]{1,0:T(8,128)(2,1)} %up_hbm.1) | copy-start | bytes 4128772
  4.8 1.3 %copy-start.2 = (bf16[168,4096]{1,0:T(8,128)(2,1)S(1)}, bf16[168,4096]{1,0:T(8,128)(2,1)}, u32[]{:S(2)}) copy-start(bf16[168,4096]{1,0:T(8,128)(2,1)} %down_hbm.1) | copy-start | bytes 4128772
  6.1 0.8 copy-start.3
  6.9 0.8 copy-start.4

commit v3 on v2

v3 whole, which is shorter than its diff:
```python
import functools

import jax
import jax.numpy as jnp
from jax import lax
from jax.experimental import pallas as pl
from jax.experimental.pallas import tpu as pltpu
from jax.sharding import PartitionSpec as P

EXPERTS = 4
MOST = 16
TAG = 128
LANES = 4
LAG_NEAR = 2
LAG_FAR = 3
LAG_SWAP = 3
MESH = pl.DeviceIdType.MESH
F32 = jnp.float32
BF16 = jnp.bfloat16
ACROSS = (((1,), (1,)), ((), ()))
LEADING = (((0,), (0,)), ((), ()))


def aligned(index, size):
    return pl.ds(pl.multiple_of(index * size, size), size)


def kernel(
    n_ctx,
    n_exp,
    n_etp,
    tok_hbm,
    grad_hbm,
    weight_hbm,
    routes_hbm,
    gate_hbm,
    up_hbm,
    down_hbm,
    d_tok_ref,
    d_gate_ref,
    d_up_ref,
    d_down_ref,
    grad_vmem,
    weight_vmem,
    routes_vmem,
    raw,
    raw_swap,
    x,
    x_swap,
    w_gate,
    w_up,
    w_down,
    acts,
    pair_out,
    pair_in,
    far_out,
    far_in,
    near_sum,
    near_out,
    near_in,
    home_out,
    home_in,
    w_sem,
    swap_send,
    swap_recv,
    z_send,
    z_recv,
    zs_send,
    zs_recv,
    x_send,
    x_recv,
    xs_send,
    xs_recv,
    y_send,
    y_recv,
    pair_send,
    pair_recv,
    far_send,
    far_recv,
    near_send,
    near_recv,
    home_send,
    home_recv,
):
    rows, feats = grad_vmem.shape
    hid = w_gate.shape[0]
    half = rows // 2
    n_x = n_etp // 2
    group_split = n_exp // EXPERTS
    chunks = n_exp // 2
    slots = n_exp * MOST
    c = lax.axis_index("ctx")
    z = lax.axis_index("exp")
    t = lax.axis_index("etp")
    xx = t // 2
    core = t % 2
    sib = t + 1 - 2 * core
    expert = z // group_split

    def along_x(step):
        return ((xx + step) % n_x) * 2 + core

    right, left, far = along_x(1), along_x(n_x - 1), along_x(2)
    z_next, z_prev = (z + 1) % n_exp, (z + n_exp - 1) % n_exp
    y_next, y_prev = (c + 1) % n_ctx, (c + n_ctx - 1) % n_ctx

    barrier = pltpu.get_barrier_semaphore()
    partners = [
        {"etp": right},
        {"etp": left},
        {"etp": sib},
        {"ctx": y_next},
        {"ctx": y_prev},
        {"exp": z_next},
        {"exp": z_prev},
    ]
    for partner in partners:
        pl.semaphore_signal(barrier, inc=1, device_id=partner, device_id_type=MESH)

    mirror = {"ctx": t, "etp": c}

    @pl.when(c != t)
    def _():
        pl.semaphore_signal(barrier, inc=1, device_id=mirror, device_id_type=MESH)

    small = [
        (tok_hbm, raw.at[pl.ds(0, rows), pl.ds(0, feats)]),
        (grad_hbm, grad_vmem),
        (weight_hbm, weight_vmem),
        (routes_hbm, routes_vmem),
    ]
    loads = [
        pltpu.make_async_copy(src, dst, w_sem.at[i])
        for i, (src, dst) in enumerate(
            small + [(gate_hbm, w_gate), (up_hbm, w_up), (down_hbm, w_down)]
        )
    ]
    for load in loads:
        load.start()
    for load in loads[: len(small)]:
        load.wait()

    square = (rows, rows)
    to_row = lax.broadcasted_iota(jnp.int32, square, 0)
    to_col = lax.broadcasted_iota(jnp.int32, square, 1)

    def as_column(row):
        return jnp.sum(jnp.where(to_row == to_col, row, jnp.zeros_like(row)), axis=1, keepdims=True)

    expert_col = as_column(routes_vmem[...].astype(F32))
    scale = as_column(weight_vmem[...])
    lane = lax.broadcasted_iota(jnp.int32, (rows, TAG), 1).astype(F32)
    one_hot = jnp.where(lane == expert_col, 1.0, 0.0)
    earlier = jnp.where(to_row > to_col, 1.0, 0.0).astype(BF16)
    before = jnp.dot(earlier, one_hot.astype(BF16), preferred_element_type=F32)
    rank = jnp.sum(before * one_hot, axis=1, keepdims=True)
    position = expert_col * MOST + rank
    raw[:rows, feats : 2 * feats] = (scale * grad_vmem[...].astype(F32)).astype(BF16)
    raw[:rows, 2 * feats :] = jnp.broadcast_to(position, (rows, TAG)).astype(BF16)

    @pl.when(c != t)
    def _():
        pl.semaphore_wait(barrier, len(partners) + 1)

    @pl.when(c == t)
    def _():
        pl.semaphore_wait(barrier, len(partners))

    def send(src, dst, send_sem, recv_sem, target):
        return pltpu.make_async_remote_copy(
            src_ref=src,
            dst_ref=dst,
            send_sem=send_sem,
            recv_sem=recv_sem,
            device_id=target,
            device_id_type=MESH,
        )

    def swap_copy():
        return send(
            raw.at[pl.ds(0, rows)], raw_swap.at[pl.ds(0, rows)], swap_send, swap_recv, mirror
        )

    def raw_half(block, part):
        return raw.at[aligned(2 * block + part, half)]

    def z_copy(src, dst, part, target):
        return send(
            raw_half(src, part),
            raw_half(dst, part),
            z_send.at[dst, part],
            z_recv.at[dst, part],
            {"exp": target},
        )

    for part in range(2):
        z_copy(0, 1, part, z_next).start()
        z_copy(0, 2, part, z_prev).start()

    @pl.when(c != t)
    def _():
        swap_copy().start()

    @pl.when(c == t)
    def _():
        raw_swap[:rows, :] = raw[:rows, :]

    def zs_copy(src, dst, target):
        return send(
            raw_swap.at[aligned(src, rows)],
            raw_swap.at[aligned(dst, rows)],
            zs_send.at[dst],
            zs_recv.at[dst],
            {"exp": target},
        )

    chunk_rows = 2 * MOST
    swap_rows = 4 * MOST
    swap_chunks = chunks // 2

    def piece(k, owner):
        return x.at[:, aligned(k, chunk_rows), aligned(owner, feats)]

    def piece_of(kind, k, owner):
        return x.at[kind, aligned(k, chunk_rows), aligned(owner, feats)]

    def swap_piece(k, owner):
        return x_swap.at[:, aligned(owner * swap_chunks + k, swap_rows), :]

    def swap_piece_of(kind, k, owner):
        return x_swap.at[kind, aligned(owner * swap_chunks + k, swap_rows), :]

    def gather(whole, part, send_sem, recv_sem):
        turn = 1 - 2 * core

        def copy(which, k):
            ref, target = (
                lambda: (whole(k, t), right),
                lambda: (whole(k, t), left),
                lambda: (whole(k, t), sib),
                lambda: (part(0, k, left), right),
                lambda: (part(1, k, right), left),
                lambda: (whole(k, left), sib),
                lambda: (whole(k, right), sib),
                lambda: (part(0, k, far), sib),
                lambda: (part(1, k, far), sib),
            )[which]()
            return send(ref, ref, send_sem.at[which, k], recv_sem.at[which, k], {"etp": target})

        def arrive(which, k):
            ref = (
                lambda: whole(k, left),
                lambda: whole(k, right),
                lambda: whole(k, sib),
                lambda: part(0, k, far),
                lambda: part(1, k, far),
                lambda: whole(k, left + turn),
                lambda: whole(k, right + turn),
                lambda: part(0, k, far + turn),
                lambda: part(1, k, far + turn),
            )[which]()
            send(ref, ref, send_sem.at[which, k], recv_sem.at[which, k], {"etp": sib}).wait_recv()

        return copy, arrive

    x_copy, x_arrive = gather(piece, piece_of, x_send, x_recv)
    xs_copy, xs_arrive = gather(swap_piece, swap_piece_of, xs_send, xs_recv)

    def pass_near(copy, arrive, k):
        arrive(0, k)
        copy(3, k).start()
        copy(5, k).start()
        arrive(1, k)
        copy(4, k).start()
        copy(6, k).start()

    def pass_far(copy, arrive, k):
        arrive(3, k)
        copy(7, k).start()
        arrive(4, k)
        copy(8, k).start()

    def finish(copy, arrive, k):
        for which in (2, 5, 6, 7, 8):
            arrive(which, k)
        for which in range(9):
            copy(which, k).wait_send()

    pick_row = lax.broadcasted_iota(jnp.int32, (2 * rows, 2 * MOST), 0)
    pick_lane = lax.broadcasted_iota(jnp.int32, (2 * rows, 2 * MOST), 1)

    def choose(blocks, k):
        block = blocks[aligned(k, 2 * rows), :]
        tag = block[:, 2 * feats : 2 * feats + 2 * MOST].astype(jnp.int32) - expert * MOST
        spot = jnp.where(pick_row >= rows, tag + MOST, tag)
        pick = jnp.where((tag >= 0) & (tag < MOST) & (spot == pick_lane), 1.0, 0.0).astype(BF16)
        return lax.dot_general(
            pick, block[:, : 2 * feats], LEADING, preferred_element_type=F32
        ).astype(BF16)

    def dispatch(i, carry):
        @pl.when(i < chunks)
        def _():
            forth, back = 2 * i + 1, 2 * i + 2
            for part in range(2):
                z_copy(forth, forth, part, z_next).wait_recv()

                @pl.when(i < chunks - 1)
                def _():
                    z_copy(forth, forth + 2, part, z_next).start()
                    z_copy(back, back, part, z_prev).wait_recv()

                @pl.when(i < chunks - 2)
                def _():
                    z_copy(back, back + 2, part, z_prev).start()

            chosen = choose(raw, i)
            x[0, aligned(i, chunk_rows), aligned(t, feats)] = chosen[:, :feats]
            x[1, aligned(i, chunk_rows), aligned(t, feats)] = chosen[:, feats:]
            for which in range(3):
                x_copy(which, i).start()

        @pl.when((i >= LAG_NEAR) & (i < chunks + LAG_NEAR))
        def _():
            pass_near(x_copy, x_arrive, i - LAG_NEAR)

        @pl.when(i >= LAG_FAR)
        def _():
            pass_far(x_copy, x_arrive, i - LAG_FAR)

        @pl.when(i == LAG_SWAP - 1)
        def _():
            @pl.when(c != t)
            def _():
                swap_copy().wait_recv()

            zs_copy(0, 1, z_next).start()
            zs_copy(0, 2, z_prev).start()

        @pl.when(i >= LAG_SWAP)
        def _():
            k = i - LAG_SWAP
            forth, back = 2 * k + 1, 2 * k + 2
            zs_copy(forth, forth, z_next).wait_recv()

            @pl.when(k < chunks - 1)
            def _():
                zs_copy(forth, forth + 2, z_next).start()
                zs_copy(back, back, z_prev).wait_recv()

            @pl.when(k < chunks - 2)
            def _():
                zs_copy(back, back + 2, z_prev).start()

            chosen = choose(raw_swap, k)
            x_swap[0, aligned(t * chunks + k, chunk_rows), :] = chosen[:, :feats]
            x_swap[1, aligned(t * chunks + k, chunk_rows), :] = chosen[:, feats:]

            @pl.when(k % 2 == 1)
            def _():
                for which in range(3):
                    xs_copy(which, k // 2).start()

        return carry

    lax.fori_loop(0, chunks + LAG_FAR, dispatch, 0)

    def gathered(k, carry):
        finish(x_copy, x_arrive, k)
        return carry

    lax.fori_loop(0, chunks, gathered, 0)
    for load in loads[len(small) :]:
        load.wait()

    tok_all, grad_all = x[0], x[1]
    gate = lax.dot_general(w_gate[...], tok_all, ACROSS, preferred_element_type=F32)
    up = lax.dot_general(w_up[...], tok_all, ACROSS, preferred_element_type=F32)
    d_hidden = lax.dot_general(w_down[...], grad_all, ACROSS, preferred_element_type=F32)
    sig = jax.nn.sigmoid(gate)
    activated = gate * sig
    hidden = activated * up
    d_gate = d_hidden * up * sig * (1.0 + gate * (1.0 - sig))
    d_up = d_hidden * activated
    acts_rows = acts.shape[0]
    acts[:, aligned(c, slots)] = jnp.concatenate(
        [d_gate, d_up, hidden, jnp.zeros((acts_rows - 3 * hid, slots), F32)], axis=0
    ).astype(BF16)
    wide = -(-hid // 128) * 128
    fill = jnp.zeros((wide - hid, slots), F32)
    gate_act = jnp.concatenate([d_gate, fill], axis=0).T.astype(BF16)[:, :hid]
    up_act = jnp.concatenate([d_up, fill], axis=0).T.astype(BF16)[:, :hid]

    lane_rows = acts_rows // LANES

    full_hops = (n_ctx - 1) // 2

    def y_copy(side, hop, lane_of):
        owner = (c + hop) % n_ctx if side else (c + n_ctx - hop) % n_ctx
        ref = acts.at[pl.ds(lane_of * lane_rows, lane_rows), aligned(owner, slots)]
        return send(
            ref,
            ref,
            y_send.at[side, hop, lane_of],
            y_recv.at[side, hop, lane_of],
            {"ctx": y_prev if side else y_next},
        )

    def y_arrive(side, hop, lane_of):
        owner = (c + hop + 1) % n_ctx if side else (c + n_ctx - hop - 1) % n_ctx
        ref = acts.at[pl.ds(lane_of * lane_rows, lane_rows), aligned(owner, slots)]
        send(
            ref,
            ref,
            y_send.at[side, hop, lane_of],
            y_recv.at[side, hop, lane_of],
            {"ctx": y_prev if side else y_next},
        ).wait_recv()

    def y_order(hop):
        if hop < full_hops:
            return [(side, lane_of) for lane_of in range(LANES) for side in range(2)]
        return [(side, 2 * lane_of + side) for lane_of in range(LANES // 2) for side in range(2)]

    def y_hop(hop):
        sends = y_order(hop) if hop <= full_hops else []
        waits = y_order(hop - 1) if hop > 0 else []
        for which in waits or sends:
            if which in waits:
                y_arrive(which[0], hop - 1, which[1])
            if which in sends:
                y_copy(which[0], hop, which[1]).start()

    def slot_part(owner):
        cols = aligned(owner, feats)
        return jnp.dot(gate_act, w_gate[:, cols], preferred_element_type=F32) + jnp.dot(
            up_act, w_up[:, cols], preferred_element_type=F32
        )

    def pair_copy(i):
        return send(
            pair_out.at[i], pair_in.at[i], pair_send.at[i], pair_recv.at[i], {"etp": sib}
        )

    middle = slots // 2

    def far_copy(side):
        return send(
            far_out.at[pl.ds(side * middle, middle)],
            far_in.at[side],
            far_send.at[side],
            far_recv.at[side],
            {"etp": left if side else right},
        )

    def near_copy(side):
        return send(
            near_out.at[side],
            near_in.at[side],
            near_send.at[side],
            near_recv.at[side],
            {"etp": left if side else right},
        )

    def to_pair():
        for i in (2, 1, 3, 0):
            pair_out[i] = slot_part(((xx + i) % n_x) * 2 + 1 - core).astype(BF16)
            pair_copy(i).start()

    def pair_sum(i):
        value = slot_part(along_x(i))
        pair_copy(i).wait_recv()
        return value + pair_in[i].astype(F32)

    def to_far():
        far_out[...] = pair_sum(2).astype(BF16)
        far_copy(0).start()
        far_copy(1).start()
        near_sum[0] = pair_sum(1)
        near_sum[1] = pair_sum(n_x - 1)

    def to_near():
        far_copy(0).wait_recv()
        near_out[0, :middle, :] = (near_sum[0, :middle, :] + far_in[0].astype(F32)).astype(BF16)
        near_out[0, middle:, :] = near_sum[0, middle:, :].astype(BF16)
        near_copy(0).start()
        far_copy(1).wait_recv()
        near_out[1, :middle, :] = near_sum[1, :middle, :].astype(BF16)
        near_out[1, middle:, :] = (near_sum[1, middle:, :] + far_in[1].astype(F32)).astype(BF16)
        near_copy(1).start()
        near_sum[2] = pair_sum(0)

    def shift(block):
        k = (block + 1) // 2
        return -k if block % 2 else k

    def home_copy(block):
        return send(
            home_out.at[pl.ds(block * MOST, MOST)],
            home_in.at[z],
            home_send.at[block],
            home_recv.at[block],
            {"exp": (z + shift(block) + n_exp) % n_exp},
        )

    def to_home():
        near_copy(0).wait_recv()
        near_copy(1).wait_recv()
        home_out[...] = (
            near_sum[2] + near_in[0].astype(F32) + near_in[1].astype(F32)
        ).astype(BF16)
        for block in range(1, n_exp):
            home_copy(block).start()
        home_in[z] = home_out[:MOST, :]

    def at_home():
        for block in range(1, n_exp):
            source = (z - shift(block) + n_exp) % n_exp
            ref = home_in.at[source]
            send(ref, ref, home_send.at[block], home_recv.at[block], {"exp": source}).wait_recv()
        merged = []
        for e in range(EXPERTS):
            value = home_in[e * group_split].astype(F32)
            for j in range(1, group_split):
                value = value + home_in[e * group_split + j].astype(F32)
            merged.append(value)
        merged = jnp.concatenate(merged, axis=0).astype(BF16)
        spots = EXPERTS * MOST
        place = jnp.where(
            lax.broadcasted_iota(jnp.int32, (rows, spots), 1) == position.astype(jnp.int32), 1.0, 0.0
        ).astype(BF16)
        d_tok_ref[...] = jnp.dot(place, merged, preferred_element_type=F32).astype(BF16)

    def swap_near(k, carry):
        pass_near(xs_copy, xs_arrive, k)
        return carry

    def swap_far(k, carry):
        pass_far(xs_copy, xs_arrive, k)
        return carry

    def swap_finish(k, carry):
        finish(xs_copy, xs_arrive, k)
        return carry

    y_hop(0)
    to_pair()
    to_far()
    y_hop(1)
    to_near()
    lax.fori_loop(0, swap_chunks, swap_near, 0)
    y_hop(2)
    to_home()
    lax.fori_loop(0, swap_chunks, swap_far, 0)
    y_hop(3)
    lax.fori_loop(0, swap_chunks, swap_finish, 0)
    y_hop(4)
    d_gate_ref[...] = jnp.dot(acts[:hid, :], x_swap[0], preferred_element_type=F32).astype(BF16)
    d_up_ref[...] = jnp.dot(
        acts[hid : 2 * hid, :], x_swap[0], preferred_element_type=F32
    ).astype(BF16)
    d_down_ref[...] = jnp.dot(
        acts[2 * hid : 3 * hid, :], x_swap[1], preferred_element_type=F32
    ).astype(BF16)
    at_home()

    @pl.when(c != t)
    def _():
        swap_copy().wait_send()

    for block in range(1, n_exp):
        for part in range(2):
            z_copy(block, block, part, z_next).wait_send()
        zs_copy(block, block, z_next).wait_send()
        home_copy(block).wait_send()
    for hop in range(full_hops + 1):
        for side, lane_of in y_order(hop):
            y_copy(side, hop, lane_of).wait_send()
    for i in range(n_x):
        pair_copy(i).wait_send()
    for side in range(2):
        far_copy(side).wait_send()
        near_copy(side).wait_send()


def hand_over(*refs):
    count = len(refs) // 2
    for i in range(count):
        refs[count + i][...] = refs[i][...]


def on_device(tokens, grad_out, route_weight, routes, w_gate, w_up, w_down):
    n_ctx, n_exp, n_etp = (lax.axis_size(name) for name in ("ctx", "exp", "etp"))
    rows, feats = tokens.shape
    hid, full = w_gate.shape
    slots = n_exp * MOST
    n_x = n_etp // 2
    chunks = n_exp // 2
    acts_rows = -(-3 * hid // (16 * LANES)) * 16 * LANES
    vmem = pl.BlockSpec(memory_space=pltpu.VMEM)
    hbm = pl.BlockSpec(memory_space=pl.ANY)
    dma = pltpu.SemaphoreType.DMA
    hops = n_ctx // 2
    grad_shape = jax.ShapeDtypeStruct((hid, feats), BF16)
    out_shape = (jax.ShapeDtypeStruct((rows, feats), BF16), grad_shape, grad_shape, grad_shape)
    results = pl.pallas_call(
        functools.partial(kernel, n_ctx, n_exp, n_etp),
        out_shape=out_shape,
        in_specs=[hbm] * 7,
        out_specs=(vmem,) * 4,
        scratch_shapes=[
            pltpu.VMEM((rows, feats), BF16),
            pltpu.VMEM((1, rows), F32),
            pltpu.VMEM((1, rows), jnp.int32),
            pltpu.VMEM((n_exp * rows, 2 * feats + TAG), BF16),
            pltpu.VMEM((n_exp * rows, 2 * feats + TAG), BF16),
            pltpu.VMEM((2, slots, full), BF16),
            pltpu.VMEM((2, n_ctx * slots, feats), BF16),
            pltpu.VMEM((hid, full), BF16),
            pltpu.VMEM((hid, full), BF16),
            pltpu.VMEM((hid, full), BF16),
            pltpu.VMEM((acts_rows, n_ctx * slots), BF16),
            pltpu.VMEM((n_x, slots, feats), BF16),
            pltpu.VMEM((n_x, slots, feats), BF16),
            pltpu.VMEM((slots, feats), BF16),
            pltpu.VMEM((2, slots // 2, feats), BF16),
            pltpu.VMEM((3, slots, feats), F32),
            pltpu.VMEM((2, slots, feats), BF16),
            pltpu.VMEM((2, slots, feats), BF16),
            pltpu.VMEM((slots, feats), BF16),
            pltpu.VMEM((n_exp, MOST, feats), BF16),
            dma((7,)),
            dma,
            dma,
            dma((n_exp, 2)),
            dma((n_exp, 2)),
            dma((n_exp,)),
            dma((n_exp,)),
            dma((9, chunks)),
            dma((9, chunks)),
            dma((9, chunks // 2)),
            dma((9, chunks // 2)),
            dma((2, hops, LANES)),
            dma((2, hops, LANES)),
            dma((n_x,)),
            dma((n_x,)),
            dma((2,)),
            dma((2,)),
            dma((2,)),
            dma((2,)),
            dma((n_exp,)),
            dma((n_exp,)),
        ],
        compiler_params=pltpu.CompilerParams(
            collective_id=0, has_side_effects=True, vmem_limit_bytes=60 * 1024 * 1024
        ),
        name="expert_backward",
    )(tokens, grad_out, route_weight.reshape(1, rows), routes.reshape(1, rows), w_gate, w_up, w_down)
    return pl.pallas_call(
        hand_over,
        out_shape=out_shape,
        in_specs=[vmem] * 4,
        out_specs=(vmem,) * 4,
        name="hand_over",
    )(*results)


def solution(mesh):
    in_specs = (
        P(("ctx", "exp"), "etp"),
        P(("ctx", "exp"), "etp"),
        P(("ctx", "exp"), None),
        P(("ctx", "exp"), None),
        P(("exp", "etp"), None),
        P(("exp", "etp"), None),
        P(("exp", "etp"), None),
    )
    out_specs = (
        P(("ctx", "exp"), "etp"),
        P(("exp", "etp"), "ctx"),
        P(("exp", "etp"), "ctx"),
        P(("exp", "etp"), "ctx"),
    )
    return jax.shard_map(
        on_device, mesh=mesh, in_specs=in_specs, out_specs=out_specs, check_vma=False
    )
```

time: 120 us -> 104 us (0.87)
  the two profiles are of different devices: /device:TPU:1 before, /device:TPU:8 now
where the time goes in v3:
time: 104 us
  Pallas kernels  103 us (99%)
    pallas_call x1, Pallas kernels, on_device(): pl.pallas_call(functools.partial(kernel, n_ctx, n_exp, n_etp), out_shape=...  101 us

profile of v3, /device:TPU:8, one launch (start us, length us, event | category | flops | bytes accessed | tf_op | source)
XLA Modules:
  0.0 103.9 jit_solution(7083779670190315445)
XLA Ops:
  0.6 101.3 %expert_backward.1 = (bf16[32,512]{1,0:T(8,128)(2,1)}, bf16[168,512]{1,0:T(8,128)(2,1)}, bf16[168,512]{1,0:T(8,128)(2,1)}, bf16[168,512]{1,0:T(8,128)(2,1)}) custom-call(bf16[32,512]{1,0:T(8,128)(2,1)} %tok_hbm.1, bf16[32,512]{1,0:T(8,128)(2,1)} %grad_hbm.1, f32[1,32]{1,0:T(1,128)} %bitcast.2, s32[1,32]{1,0:T(1,128)} %bitcast.3, bf16[168,4096]{1,0:T(8,128)(2,1)} %gate_hbm.1, ...), custom_call_target="tpu_custom_call" | custom-call | tf_op jit(solution)/shard_map/expert_backward/pallas_call | solution.py:606
  101.9 1.9 %hand_over.1 = (bf16[32,512]{1,0:T(8,128)(2,1)}, bf16[168,512]{1,0:T(8,128)(2,1)}, bf16[168,512]{1,0:T(8,128)(2,1)}, bf16[168,512]{1,0:T(8,128)(2,1)}) custom-call(bf16[32,512]{1,0:T(8,128)(2,1)} %get-tuple-element.8.refs_0_, bf16[168,512]{1,0:T(8,128)(2,1)} %get-tuple-element.9.refs_1_, bf16[168,512]{1,0:T(8,128)(2,1)} %get-tuple-element.10.refs_2_, ...), custom_call_target="tpu_custom_call" | custom-call | tf_op jit(solution)/shard_map/hand_over/pallas_call | solution.py:659

commit v4 on v3

--- a/solution.py
+++ b/solution.py
@@ -10,8 +10,9 @@
 EXPERTS = 4
 MOST = 16
 TAG = 128
-LANES = 4
-LAG_NEAR = 2
+LANES = 2
+PARTS = 2
+LAG_NEAR = 1
 LAG_FAR = 3
 LAG_SWAP = 3
 MESH = pl.DeviceIdType.MESH
@@ -19,6 +20,12 @@
 BF16 = jnp.bfloat16
 ACROSS = (((1,), (1,)), ((), ()))
 LEADING = (((0,), (0,)), ((), ()))
+
+
+def when(condition):
+    if isinstance(condition, bool):
+        return lambda body: body() if condition else None
+    return pl.when(condition)
 
 
 def aligned(index, size):
@@ -298,29 +305,49 @@
             pick, block[:, : 2 * feats], LEADING, preferred_element_type=F32
         ).astype(BF16)
 
+    def swap_step(k):
+        forth, back = 2 * k + 1, 2 * k + 2
+        zs_copy(forth, forth, z_next).wait_recv()
+
+        @when(k < chunks - 1)
+        def _():
+            zs_copy(forth, forth + 2, z_next).start()
+            zs_copy(back, back, z_prev).wait_recv()
+
+        @when(k < chunks - 2)
+        def _():
+            zs_copy(back, back + 2, z_prev).start()
+
+        chosen = choose(raw_swap, k)
+        x_swap[0, aligned(t * chunks + k, chunk_rows), :] = chosen[:, :feats]
+        x_swap[1, aligned(t * chunks + k, chunk_rows), :] = chosen[:, feats:]
+
+        @when(k % 2 == 1)
+        def _():
+            for which in range(3):
+                xs_copy(which, k // 2).start()
+
     def dispatch(i, carry):
-        @pl.when(i < chunks)
-        def _():
-            forth, back = 2 * i + 1, 2 * i + 2
-            for part in range(2):
-                z_copy(forth, forth, part, z_next).wait_recv()
-
-                @pl.when(i < chunks - 1)
-                def _():
-                    z_copy(forth, forth + 2, part, z_next).start()
-                    z_copy(back, back, part, z_prev).wait_recv()
-
-                @pl.when(i < chunks - 2)
-                def _():
-                    z_copy(back, back + 2, part, z_prev).start()
-
-            chosen = choose(raw, i)
-            x[0, aligned(i, chunk_rows), aligned(t, feats)] = chosen[:, :feats]
-            x[1, aligned(i, chunk_rows), aligned(t, feats)] = chosen[:, feats:]
-            for which in range(3):
-                x_copy(which, i).start()
-
-        @pl.when((i >= LAG_NEAR) & (i < chunks + LAG_NEAR))
+        forth, back = 2 * i + 1, 2 * i + 2
+        for part in range(2):
+            z_copy(forth, forth, part, z_next).wait_recv()
+
+            @pl.when(i < chunks - 1)
+            def _():
+                z_copy(forth, forth + 2, part, z_next).start()
+                z_copy(back, back, part, z_prev).wait_recv()
+
+            @pl.when(i < chunks - 2)
+            def _():
+                z_copy(back, back + 2, part, z_prev).start()
+
+        chosen = choose(raw, i)
+        x[0, aligned(i, chunk_rows), aligned(t, feats)] = chosen[:, :feats]
+        x[1, aligned(i, chunk_rows), aligned(t, feats)] = chosen[:, feats:]
+        for which in range(3):
+            x_copy(which, i).start()
+
+        @pl.when(i >= LAG_NEAR)
         def _():
             pass_near(x_copy, x_arrive, i - LAG_NEAR)
 
@@ -339,156 +366,147 @@
 
         @pl.when(i >= LAG_SWAP)
         def _():
-            k = i - LAG_SWAP
-            forth, back = 2 * k + 1, 2 * k + 2
-            zs_copy(forth, forth, z_next).wait_recv()
-
-            @pl.when(k < chunks - 1)
-            def _():
-                zs_copy(forth, forth + 2, z_next).start()
-                zs_copy(back, back, z_prev).wait_recv()
-
-            @pl.when(k < chunks - 2)
-            def _():
-                zs_copy(back, back + 2, z_prev).start()
-
-            chosen = choose(raw_swap, k)
-            x_swap[0, aligned(t * chunks + k, chunk_rows), :] = chosen[:, :feats]
-            x_swap[1, aligned(t * chunks + k, chunk_rows), :] = chosen[:, feats:]
-
-            @pl.when(k % 2 == 1)
-            def _():
-                for which in range(3):
-                    xs_copy(which, k // 2).start()
+            swap_step(i - LAG_SWAP)
 
         return carry
 
-    lax.fori_loop(0, chunks + LAG_FAR, dispatch, 0)
+    lax.fori_loop(0, chunks, dispatch, 0)
 
     def gathered(k, carry):
         finish(x_copy, x_arrive, k)
         return carry
 
-    lax.fori_loop(0, chunks, gathered, 0)
-    for load in loads[len(small) :]:
-        load.wait()
-
-    tok_all, grad_all = x[0], x[1]
-    gate = lax.dot_general(w_gate[...], tok_all, ACROSS, preferred_element_type=F32)
-    up = lax.dot_general(w_up[...], tok_all, ACROSS, preferred_element_type=F32)
-    d_hidden = lax.dot_general(w_down[...], grad_all, ACROSS, preferred_element_type=F32)
-    sig = jax.nn.sigmoid(gate)
-    activated = gate * sig
-    hidden = activated * up
-    d_gate = d_hidden * up * sig * (1.0 + gate * (1.0 - sig))
-    d_up = d_hidden * activated
+
     acts_rows = acts.shape[0]
-    acts[:, aligned(c, slots)] = jnp.concatenate(
-        [d_gate, d_up, hidden, jnp.zeros((acts_rows - 3 * hid, slots), F32)], axis=0
-    ).astype(BF16)
+    part_slots = slots // PARTS
     wide = -(-hid // 128) * 128
-    fill = jnp.zeros((wide - hid, slots), F32)
-    gate_act = jnp.concatenate([d_gate, fill], axis=0).T.astype(BF16)[:, :hid]
-    up_act = jnp.concatenate([d_up, fill], axis=0).T.astype(BF16)[:, :hid]
+    fill = jnp.zeros((wide - hid, part_slots), F32)
+    turned = {}
+
+    def forward(part):
+        here = pl.ds(part * part_slots, part_slots)
+        gate = lax.dot_general(w_gate[...], x[0, here, :], ACROSS, preferred_element_type=F32)
+        up = lax.dot_general(w_up[...], x[0, here, :], ACROSS, preferred_element_type=F32)
+        d_hidden = lax.dot_general(w_down[...], x[1, here, :], ACROSS, preferred_element_type=F32)
+        sig = jax.nn.sigmoid(gate)
+        activated = gate * sig
+        hidden = activated * up
+        d_gate = d_hidden * up * sig * (1.0 + gate * (1.0 - sig))
+        d_up = d_hidden * activated
+        acts[:, aligned(c * PARTS + part, part_slots)] = jnp.concatenate(
+            [d_gate, d_up, hidden, jnp.zeros((acts_rows - 3 * hid, part_slots), F32)], axis=0
+        ).astype(BF16)
+        turned[part] = tuple(
+            jnp.concatenate([value, fill], axis=0).T.astype(BF16)[:, :hid]
+            for value in (d_gate, d_up)
+        )
 
     lane_rows = acts_rows // LANES
 
     full_hops = (n_ctx - 1) // 2
 
-    def y_copy(side, hop, lane_of):
-        owner = (c + hop) % n_ctx if side else (c + n_ctx - hop) % n_ctx
-        ref = acts.at[pl.ds(lane_of * lane_rows, lane_rows), aligned(owner, slots)]
+    def y_block(part, owner, lane_of):
+        return acts.at[
+            pl.ds(lane_of * lane_rows, lane_rows), aligned(owner * PARTS + part, part_slots)
+        ]
+
+    def y_send_of(part, side, hop, lane_of, ref):
         return send(
             ref,
             ref,
-            y_send.at[side, hop, lane_of],
-            y_recv.at[side, hop, lane_of],
+            y_send.at[part, side, hop, lane_of],
+            y_recv.at[part, side, hop, lane_of],
             {"ctx": y_prev if side else y_next},
         )
 
-    def y_arrive(side, hop, lane_of):
+    def y_copy(part, side, hop, lane_of):
+        owner = (c + hop) % n_ctx if side else (c + n_ctx - hop) % n_ctx
+        return y_send_of(part, side, hop, lane_of, y_block(part, owner, lane_of))
+
+    def y_arrive(part, side, hop, lane_of):
         owner = (c + hop + 1) % n_ctx if side else (c + n_ctx - hop - 1) % n_ctx
-        ref = acts.at[pl.ds(lane_of * lane_rows, lane_rows), aligned(owner, slots)]
-        send(
-            ref,
-            ref,
-            y_send.at[side, hop, lane_of],
-            y_recv.at[side, hop, lane_of],
-            {"ctx": y_prev if side else y_next},
-        ).wait_recv()
+        y_send_of(part, side, hop, lane_of, y_block(part, owner, lane_of)).wait_recv()
 
     def y_order(hop):
         if hop < full_hops:
             return [(side, lane_of) for lane_of in range(LANES) for side in range(2)]
         return [(side, 2 * lane_of + side) for lane_of in range(LANES // 2) for side in range(2)]
 
-    def y_hop(hop):
+    def y_hop(part, hop):
         sends = y_order(hop) if hop <= full_hops else []
         waits = y_order(hop - 1) if hop > 0 else []
         for which in waits or sends:
             if which in waits:
-                y_arrive(which[0], hop - 1, which[1])
+                y_arrive(part, which[0], hop - 1, which[1])
             if which in sends:
-                y_copy(which[0], hop, which[1]).start()
-
-    def slot_part(owner):
+                y_copy(part, which[0], hop, which[1]).start()
+
+    def slot_part(part, owner):
         cols = aligned(owner, feats)
+        gate_act, up_act = turned[part]
         return jnp.dot(gate_act, w_gate[:, cols], preferred_element_type=F32) + jnp.dot(
             up_act, w_up[:, cols], preferred_element_type=F32
         )
 
-    def pair_copy(i):
+    def pair_copy(part, i):
         return send(
-            pair_out.at[i], pair_in.at[i], pair_send.at[i], pair_recv.at[i], {"etp": sib}
-        )
-
-    middle = slots // 2
-
-    def far_copy(side):
+            pair_out.at[part, i],
+            pair_in.at[part, i],
+            pair_send.at[part, i],
+            pair_recv.at[part, i],
+            {"etp": sib},
+        )
+
+    middle = part_slots // 2
+
+    def far_copy(part, side):
         return send(
-            far_out.at[pl.ds(side * middle, middle)],
-            far_in.at[side],
-            far_send.at[side],
-            far_recv.at[side],
+            far_out.at[part, pl.ds(side * middle, middle)],
+            far_in.at[part, side],
+            far_send.at[part, side],
+            far_recv.at[part, side],
             {"etp": left if side else right},
         )
 
-    def near_copy(side):
+    def near_copy(part, side):
         return send(
-            near_out.at[side],
-            near_in.at[side],
-            near_send.at[side],
-            near_recv.at[side],
+            near_out.at[part, side],
+            near_in.at[part, side],
+            near_send.at[part, side],
+            near_recv.at[part, side],
             {"etp": left if side else right},
         )
 
-    def to_pair():
+    def to_pair(part):
         for i in (2, 1, 3, 0):
-            pair_out[i] = slot_part(((xx + i) % n_x) * 2 + 1 - core).astype(BF16)
-            pair_copy(i).start()
-
-    def pair_sum(i):
-        value = slot_part(along_x(i))
-        pair_copy(i).wait_recv()
-        return value + pair_in[i].astype(F32)
-
-    def to_far():
-        far_out[...] = pair_sum(2).astype(BF16)
-        far_copy(0).start()
-        far_copy(1).start()
-        near_sum[0] = pair_sum(1)
-        near_sum[1] = pair_sum(n_x - 1)
-
-    def to_near():
-        far_copy(0).wait_recv()
-        near_out[0, :middle, :] = (near_sum[0, :middle, :] + far_in[0].astype(F32)).astype(BF16)
-        near_out[0, middle:, :] = near_sum[0, middle:, :].astype(BF16)
-        near_copy(0).start()
-        far_copy(1).wait_recv()
-        near_out[1, :middle, :] = near_sum[1, :middle, :].astype(BF16)
-        near_out[1, middle:, :] = (near_sum[1, middle:, :] + far_in[1].astype(F32)).astype(BF16)
-        near_copy(1).start()
-        near_sum[2] = pair_sum(0)
+            owner = ((xx + i) % n_x) * 2 + 1 - core
+            pair_out[part, i] = slot_part(part, owner).astype(BF16)
+            pair_copy(part, i).start()
+
+    def pair_sum(part, i):
+        value = slot_part(part, along_x(i))
+        pair_copy(part, i).wait_recv()
+        return value + pair_in[part, i].astype(F32)
+
+    def to_far(part):
+        far_out[part] = pair_sum(part, 2).astype(BF16)
+        far_copy(part, 0).start()
+        far_copy(part, 1).start()
+        near_sum[part, 0] = pair_sum(part, 1)
+        near_sum[part, 1] = pair_sum(part, n_x - 1)
+
+    def to_near(part):
+        for side in range(2):
+            far_copy(part, side).wait_recv()
+            low, high = near_sum[part, side, :middle, :], near_sum[part, side, middle:, :]
+            if side:
+                high = high + far_in[part, side].astype(F32)
+            else:
+                low = low + far_in[part, side].astype(F32)
+            near_out[part, side, :middle, :] = low.astype(BF16)
+            near_out[part, side, middle:, :] = high.astype(BF16)
+            near_copy(part, side).start()
+        near_sum[part, 2] = pair_sum(part, 0)
 
     def shift(block):
         k = (block + 1) // 2
@@ -503,15 +521,18 @@
             {"exp": (z + shift(block) + n_exp) % n_exp},
         )
 
-    def to_home():
-        near_copy(0).wait_recv()
-        near_copy(1).wait_recv()
-        home_out[...] = (
-            near_sum[2] + near_in[0].astype(F32) + near_in[1].astype(F32)
+    def to_home(part):
+        near_copy(part, 0).wait_recv()
+        near_copy(part, 1).wait_recv()
+        home_out[pl.ds(part * part_slots, part_slots), :] = (
+            near_sum[part, 2] + near_in[part, 0].astype(F32) + near_in[part, 1].astype(F32)
         ).astype(BF16)
-        for block in range(1, n_exp):
-            home_copy(block).start()
-        home_in[z] = home_out[:MOST, :]
+        per = n_exp // PARTS
+        for block in range(per * part, per * (part + 1)):
+            if block == 0:
+                home_in[z] = home_out[:MOST, :]
+            else:
+                home_copy(block).start()
 
     def at_home():
         for block in range(1, n_exp):
@@ -531,30 +552,65 @@
         ).astype(BF16)
         d_tok_ref[...] = jnp.dot(place, merged, preferred_element_type=F32).astype(BF16)
 
-    def swap_near(k, carry):
-        pass_near(xs_copy, xs_arrive, k)
-        return carry
-
-    def swap_far(k, carry):
-        pass_far(xs_copy, xs_arrive, k)
-        return carry
-
-    def swap_finish(k, carry):
-        finish(xs_copy, xs_arrive, k)
-        return carry
-
-    y_hop(0)
-    to_pair()
-    to_far()
-    y_hop(1)
-    to_near()
-    lax.fori_loop(0, swap_chunks, swap_near, 0)
-    y_hop(2)
-    to_home()
-    lax.fori_loop(0, swap_chunks, swap_far, 0)
-    y_hop(3)
-    lax.fori_loop(0, swap_chunks, swap_finish, 0)
-    y_hop(4)
+    def weights_here():
+        for load in loads[len(small) :]:
+            load.wait()
+
+    def gather_done(part):
+        per = chunks // PARTS
+        lax.fori_loop(per * part, per * (part + 1), gathered, 0)
+
+    def swap_done():
+        for k in range(swap_chunks):
+            finish(xs_copy, xs_arrive, k)
+
+    near = functools.partial(pass_near, x_copy, x_arrive)
+    far_on = functools.partial(pass_far, x_copy, x_arrive)
+    swap_near = functools.partial(pass_near, xs_copy, xs_arrive)
+    swap_far = functools.partial(pass_far, xs_copy, xs_arrive)
+    plan = [
+        (far_on, 5),
+        (weights_here,),
+        (gather_done, 0),
+        (forward, 0),
+        (y_hop, 0, 0),
+        (near, 7),
+        (to_pair, 0),
+        (far_on, 6),
+        (swap_step, 5),
+        (to_far, 0),
+        (far_on, 7),
+        (swap_near, 0),
+        (swap_step, 6),
+        (gather_done, 1),
+        (to_near, 0),
+        (forward, 1),
+        (y_hop, 1, 0),
+        (to_pair, 1),
+        (swap_step, 7),
+        (y_hop, 0, 1),
+        (to_home, 0),
+        (to_far, 1),
+        (swap_near, 1),
+        (swap_far, 0),
+        (y_hop, 1, 1),
+        (to_near, 1),
+        (y_hop, 0, 2),
+        (swap_near, 2),
+        (swap_near, 3),
+        (swap_far, 1),
+        (to_home, 1),
+        (y_hop, 1, 2),
+        (y_hop, 0, 3),
+        (swap_far, 2),
+        (swap_far, 3),
+        (y_hop, 1, 3),
+        (y_hop, 0, 4),
+        (y_hop, 1, 4),
+        (swap_done,),
+    ]
+    for stage in plan:
+        stage[0](*stage[1:])
     d_gate_ref[...] = jnp.dot(acts[:hid, :], x_swap[0], preferred_element_type=F32).astype(BF16)
     d_up_ref[...] = jnp.dot(
         acts[hid : 2 * hid, :], x_swap[0], preferred_element_type=F32
@@ -575,12 +631,14 @@
         home_copy(block).wait_send()
     for hop in range(full_hops + 1):
         for side, lane_of in y_order(hop):
-            y_copy(side, hop, lane_of).wait_send()
-    for i in range(n_x):
-        pair_copy(i).wait_send()
-    for side in range(2):
-        far_copy(side).wait_send()
-        near_copy(side).wait_send()
+            for part in range(PARTS):
+                y_copy(part, side, hop, lane_of).wait_send()
+    for part in range(PARTS):
+        for i in range(n_x):
+            pair_copy(part, i).wait_send()
+        for side in range(2):
+            far_copy(part, side).wait_send()
+            near_copy(part, side).wait_send()
 
 
 def hand_over(*refs):
@@ -601,6 +659,7 @@
     hbm = pl.BlockSpec(memory_space=pl.ANY)
     dma = pltpu.SemaphoreType.DMA
     hops = n_ctx // 2
+    part_slots = slots // PARTS
     grad_shape = jax.ShapeDtypeStruct((hid, feats), BF16)
     out_shape = (jax.ShapeDtypeStruct((rows, feats), BF16), grad_shape, grad_shape, grad_shape)
     results = pl.pallas_call(
@@ -620,13 +679,13 @@
             pltpu.VMEM((hid, full), BF16),
             pltpu.VMEM((hid, full), BF16),
             pltpu.VMEM((acts_rows, n_ctx * slots), BF16),
-            pltpu.VMEM((n_x, slots, feats), BF16),
-            pltpu.VMEM((n_x, slots, feats), BF16),
-            pltpu.VMEM((slots, feats), BF16),
-            pltpu.VMEM((2, slots // 2, feats), BF16),
-            pltpu.VMEM((3, slots, feats), F32),
-            pltpu.VMEM((2, slots, feats), BF16),
-            pltpu.VMEM((2, slots, feats), BF16),
+            pltpu.VMEM((PARTS, n_x, part_slots, feats), BF16),
+            pltpu.VMEM((PARTS, n_x, part_slots, feats), BF16),
+            pltpu.VMEM((PARTS, part_slots, feats), BF16),
+            pltpu.VMEM((PARTS, 2, part_slots // 2, feats), BF16),
+            pltpu.VMEM((PARTS, 3, part_slots, feats), F32),
+            pltpu.VMEM((PARTS, 2, part_slots, feats), BF16),
+            pltpu.VMEM((PARTS, 2, part_slots, feats), BF16),
             pltpu.VMEM((slots, feats), BF16),
             pltpu.VMEM((n_exp, MOST, feats), BF16),
             dma((7,)),
@@ -640,14 +699,14 @@
             dma((9, chunks)),
             dma((9, chunks // 2)),
             dma((9, chunks // 2)),
-            dma((2, hops, LANES)),
-            dma((2, hops, LANES)),
-            dma((n_x,)),
-            dma((n_x,)),
-            dma((2,)),
-            dma((2,)),
-            dma((2,)),
-            dma((2,)),
+            dma((PARTS, 2, hops, LANES)),
+            dma((PARTS, 2, hops, LANES)),
+            dma((PARTS, n_x)),
+            dma((PARTS, n_x)),
+            dma((PARTS, 2)),
+            dma((PARTS, 2)),
+            dma((PARTS, 2)),
+            dma((PARTS, 2)),
             dma((n_exp,)),
             dma((n_exp,)),
         ],

time: 104 us -> 95.6 us (0.919)
  the two profiles are of different devices: /device:TPU:8 before, /device:TPU:24 now
where the time goes in v4:
time: 95.6 us; the launch traced here: 95.5 us
  Pallas kernels  94.8 us (99%)
    pallas_call x1, Pallas kernels, on_device(): pl.pallas_call(functools.partial(kernel, n_ctx, n_exp, n_etp), out_shape=...  92.9 us
    pallas_call x1, Pallas kernels, on_device(): pl.pallas_call(hand_over, out_shape=out_shape, in_specs=[vmem] * 4, out_s...  1.91 us

profile of v4, /device:TPU:24, one launch (start us, length us, event | category | flops | bytes accessed | tf_op | source)
XLA Modules:
  0.0 95.5 jit_solution(15568751346692391820)
XLA Ops:
  0.6 92.9 %expert_backward.1 = (bf16[32,512]{1,0:T(8,128)(2,1)}, bf16[168,512]{1,0:T(8,128)(2,1)}, bf16[168,512]{1,0:T(8,128)(2,1)}, bf16[168,512]{1,0:T(8,128)(2,1)}) custom-call(bf16[32,512]{1,0:T(8,128)(2,1)} %tok_hbm.1, bf16[32,512]{1,0:T(8,128)(2,1)} %grad_hbm.1, f32[1,32]{1,0:T(1,128)} %bitcast.2, s32[1,32]{1,0:T(1,128)} %bitcast.3, bf16[168,4096]{1,0:T(8,128)(2,1)} %gate_hbm.1, ...), custom_call_target="tpu_custom_call" | custom-call | tf_op jit(solution)/shard_map/expert_backward/pallas_call | solution.py:665
  93.6 1.9 %hand_over.1 = (bf16[32,512]{1,0:T(8,128)(2,1)}, bf16[168,512]{1,0:T(8,128)(2,1)}, bf16[168,512]{1,0:T(8,128)(2,1)}, bf16[168,512]{1,0:T(8,128)(2,1)}) custom-call(bf16[32,512]{1,0:T(8,128)(2,1)} %get-tuple-element.8.refs_0_, bf16[168,512]{1,0:T(8,128)(2,1)} %get-tuple-element.9.refs_1_, bf16[168,512]{1,0:T(8,128)(2,1)} %get-tuple-element.10.refs_2_, ...), custom_call_target="tpu_custom_call" | custom-call | tf_op jit(solution)/shard_map/hand_over/pallas_call | solution.py:718
